TPU v7x, 32 devices: a whole 2x2x4 slice. The times are simulated.
32 devices in a mesh: ctx: 16 (over z, y, x), tp: 2 (over core).
Axes of the slice: x: 2, y: 2, z: 4, core: 2. Of those that a mesh axis runs over, the one named last changes fastest.
Arguments:
- inputs: bfloat16 [2048, 2048], P('ctx', 'tp'), may hold values from -6.5 to 6.5
- query_weight: bfloat16 [2048, 1024], P(None, 'tp'), may hold values from -0.125 to 0.125
- key_weight: bfloat16 [2048, 1024], P(None, 'tp'), may hold values from -0.125 to 0.125
- value_weight: bfloat16 [2048, 2048], P(None, 'tp'), may hold values from -0.125 to 0.125
- beta_weight: bfloat16 [2048, 16], P(None, 'tp'), may hold values from -1.5 to 1.5
- alpha_weight: bfloat16 [2048, 16], P(None, 'tp'), may hold values from -0.125 to 0.125
- query_filter: bfloat16 [4, 1024], P(None, 'tp'), may hold values from -3 to 3
- key_filter: bfloat16 [4, 1024], P(None, 'tp'), may hold values from -3 to 3
- value_filter: bfloat16 [4, 2048], P(None, 'tp'), may hold values from -3 to 3
- decay_log: float32 [16], P('tp'), may hold values from 0 to 2.77
- step_bias: float32 [16], P('tp'), may hold values from -16 to -2.3
- grad_core: bfloat16 [2048, 2048], P('ctx', 'tp'), may hold values from -6 to 6
Outputs:
- grad_inputs: bfloat16 [2048, 2048], P('ctx', 'tp')
All inputs are finite; a program needn't handle non-finite values.
Results may differ from a plain program's by a relative error of at most 0.019.
Values may be sent and summed in bfloat16 or wider, within the bound.
A program may use at most 128 MiB of HBM per device.

v0:
```python
import jax
import jax.numpy as jnp
from jax import lax
from jax.sharding import PartitionSpec as P

DH = 128
CONV = 4
GROUP = 64


EPS = 1e-06


def from_behind(value, axis, steps):
    count = lax.axis_size(axis)
    leading, last = (max(0, -steps), min(count, count - steps))
    return lax.ppermute(value, axis, [(source, source + steps) for source in range(leading, last)])


def entering(value, axis, join, neutral, backward):
    count, mine = (lax.axis_size(axis), lax.axis_index(axis))
    pieces = jax.tree.map(lambda part: lax.all_gather(part, axis), value)
    if backward:
        pieces = jax.tree.map(lambda part: part[::-1], pieces)
        mine = count - 1 - mine
    subtotal = jax.tree.map(
        lambda part, zero: jnp.full_like(part, 0) + jnp.asarray(zero, part.dtype), value, neutral
    )

    def step(position, subtotal):
        longer = join(subtotal, jax.tree.map(lambda part: part[position], pieces))
        return jax.tree.map(lambda new, old: jnp.where(position < mine, new, old), longer, subtotal)

    return lax.fori_loop(0, count - 1, step, subtotal)


def contract(form, left_arr, right_arr):
    return jnp.einsum(
        form,
        left_arr,
        right_arr,
        precision=lax.Precision.HIGHEST,
        preferred_element_type=jnp.float32,
    )


def unit_lower_inverse(strict):
    size_now = strict.shape[-1]
    identity = jnp.eye(size_now, dtype=jnp.float32)
    result = identity - strict
    power_of = contract("...ij,...jk->...ik", strict, strict)
    covered = 2
    while covered < size_now:
        result = contract("...ij,...jk->...ik", result, identity + power_of)
        power_of = contract("...ij,...jk->...ik", power_of, power_of)
        covered = covered * 2
    return result


def conv_silu(padded, weight):
    tap_count = weight.shape[0]
    length = padded.shape[0] - tap_count + 1
    running = jnp.zeros((length, padded.shape[1]), jnp.float32)
    for tap_index in range(tap_count):
        running = (
            running + weight[tap_index].astype(jnp.float32) * padded[tap_index : tap_index + length]
        )
    return jax.nn.silu(running)


def normalized(rows_in, heads_count):
    shaped = rows_in.reshape(rows_in.shape[0], heads_count, -1)
    return shaped * lax.rsqrt(jnp.sum(shaped * shaped, axis=-1, keepdims=True) + EPS)


def to_blocks(rows_in, block_count):
    return rows_in.reshape(block_count, GROUP, rows_in.shape[1], -1).transpose(0, 2, 1, 3)


def prepare(
    query_pad,
    key_pad,
    value_pad,
    beta_raw,
    alpha_raw,
    query_filter,
    key_filter,
    value_filter,
    decay_log,
    step_bias,
):
    query_act = conv_silu(query_pad, query_filter)
    key_act = conv_silu(key_pad, key_filter)
    value_act = conv_silu(value_pad, value_filter)
    length = query_act.shape[0]
    key_heads = query_act.shape[1] // DH
    value_heads = value_act.shape[1] // DH
    ratio_kv = value_heads // key_heads
    block_count = length // GROUP
    query_unit = jnp.repeat(normalized(query_act, key_heads) * DH ** (-0.5), ratio_kv, axis=1)
    key_unit = jnp.repeat(normalized(key_act, key_heads), ratio_kv, axis=1)
    query_blk = to_blocks(query_unit, block_count)
    key_blk = to_blocks(key_unit, block_count)
    value_blk = to_blocks(value_act.reshape(length, value_heads, DH), block_count)
    beta_blk = jax.nn.sigmoid(beta_raw).reshape(block_count, GROUP, value_heads).transpose(0, 2, 1)
    log_decay = -jnp.exp(decay_log) * jax.nn.softplus(alpha_raw + step_bias)
    cum_decay = jnp.cumsum(
        log_decay.reshape(block_count, GROUP, value_heads).transpose(0, 2, 1), axis=-1
    )
    row_pos = lax.broadcasted_iota(jnp.int32, (GROUP, GROUP), 0)
    col_pos = lax.broadcasted_iota(jnp.int32, (GROUP, GROUP), 1)
    lower_mask = row_pos >= col_pos
    strictly = row_pos > col_pos
    gap_log = cum_decay[..., :, None] - cum_decay[..., None, :]
    decay_ij = jnp.where(lower_mask, jnp.exp(jnp.where(lower_mask, gap_log, 0.0)), 0.0)
    key_gram = contract("nhia,nhja->nhij", key_blk, key_blk)
    strict = jnp.where(strictly, beta_blk[..., :, None] * key_gram * decay_ij, 0.0)
    inverse = unit_lower_inverse(strict)
    gamma_at = jnp.exp(cum_decay)
    value_mix = contract("nhij,nhjb->nhib", inverse, beta_blk[..., None] * value_blk)
    key_weighted = contract("nhij,nhja->nhia", inverse, (beta_blk * gamma_at)[..., None] * key_blk)
    query_scaled = gamma_at[..., None] * query_blk
    key_tail = jnp.exp(cum_decay[..., -1:] - cum_decay)[..., None] * key_blk
    mixing = contract("nhia,nhja->nhij", query_blk, key_blk) * decay_ij
    end_decay = jnp.exp(cum_decay[..., -1])
    return (query_scaled, key_weighted, value_mix, key_tail, mixing, end_decay)


def transitions(pieces):
    query_scaled, key_weighted, value_mix, key_tail, mixing, end_decay = pieces
    unit_matrix = jnp.eye(key_tail.shape[-1], dtype=jnp.float32)
    trans_step = end_decay[..., None, None] * unit_matrix - contract(
        "nhca,nhcd->nhad", key_tail, key_weighted
    )
    inject_step = contract("nhca,nhcb->nhab", key_tail, value_mix)
    return (trans_step, inject_step)


def head_outputs(pieces, starts):
    query_scaled, key_weighted, value_mix, key_tail, mixing, end_decay = pieces
    fresh = value_mix - contract("nhca,nhab->nhcb", key_weighted, starts)
    return contract("nhca,nhab->nhcb", query_scaled, starts) + contract(
        "nhij,nhjb->nhib", mixing, fresh
    )


def slab_chain(pieces):
    trans_step, inject_step = transitions(pieces)
    heads_count = trans_step.shape[1]
    width_now = trans_step.shape[2]
    unit_matrix = jnp.broadcast_to(
        jnp.eye(width_now, dtype=jnp.float32), (heads_count, width_now, width_now)
    )
    zero_state = jnp.zeros(inject_step.shape[1:], jnp.float32)

    def advance(carried, step_pair):
        product, offset = carried
        step_trans, step_inject = step_pair
        moved = (
            contract("had,hde->hae", step_trans, product),
            contract("had,hdb->hab", step_trans, offset) + step_inject,
        )
        return (moved, carried)

    (slab_trans, slab_inject), (block_trans, block_seeds) = lax.scan(
        advance, (unit_matrix, zero_state), (trans_step, inject_step)
    )
    return (block_trans, block_seeds, slab_trans, slab_inject)


def finish(pieces, block_trans, block_seeds, incoming):
    starts = contract("nhad,hdb->nhab", block_trans, incoming) + block_seeds
    return head_outputs(pieces, starts)


def compose(earlier, later):
    return (
        contract("had,hde->hae", later[0], earlier[0]),
        contract("had,hdb->hab", later[0], earlier[1]) + later[1],
    )


def add_pair(first_item, second_item):
    return first_item + second_item


def local(
    inputs,
    query_weight,
    key_weight,
    value_weight,
    beta_weight,
    alpha_weight,
    query_filter,
    key_filter,
    value_filter,
    decay_log,
    step_bias,
    grad_core,
):
    rows_here = inputs.shape[0]
    conv_lag = CONV - 1
    weights = (query_weight, key_weight, value_weight, beta_weight, alpha_weight)

    def add_rows(shard_rows):
        return tuple(
            (jnp.dot(shard_rows, weight, preferred_element_type=jnp.float32) for weight in weights)
        )

    projected = add_rows(lax.all_gather(inputs, "tp", axis=1, tiled=True))
    rounded = lax.optimization_barrier(tuple((member.astype(jnp.bfloat16) for member in projected)))
    tail_rows = from_behind(
        (
            rounded[0][rows_here - conv_lag :],
            rounded[1][rows_here - conv_lag :],
            rounded[2][rows_here - conv_lag :],
        ),
        "ctx",
        1,
    )
    primals = tuple((member.astype(jnp.float32) for member in rounded)) + tuple(
        (member.astype(jnp.float32) for member in tail_rows)
    )

    def local_pieces(
        query_rows, key_rows, value_rows, beta_raw, alpha_raw, query_prev, key_prev, value_prev
    ):
        return prepare(
            jnp.concatenate([query_prev, query_rows], 0),
            jnp.concatenate([key_prev, key_rows], 0),
            jnp.concatenate([value_prev, value_rows], 0),
            beta_raw,
            alpha_raw,
            query_filter,
            key_filter,
            value_filter,
            decay_log,
            step_bias,
        )

    pieces, pieces_back = jax.vjp(local_pieces, *primals)
    chain_out, chain_back = jax.vjp(slab_chain, pieces)
    block_trans, block_seeds, slab_trans, slab_inject = chain_out
    heads_count = slab_trans.shape[0]
    width_now = slab_trans.shape[1]
    identity = (
        jnp.broadcast_to(
            jnp.eye(width_now, dtype=jnp.float32), (heads_count, width_now, width_now)
        ),
        jnp.zeros(slab_inject.shape, jnp.float32),
    )
    grad_heads = to_blocks(
        grad_core.astype(jnp.float32).reshape(rows_here, heads_count, -1), rows_here // GROUP
    )
    incoming = entering((slab_trans, slab_inject), "ctx", compose, identity, False)[1]
    _, finish_back = jax.vjp(finish, pieces, block_trans, block_seeds, incoming)
    grad_pieces_out, grad_block_trans, grad_block_seeds, after_grad = finish_back(grad_heads)
    later_grad = entering(
        (jnp.swapaxes(slab_trans, 1, 2), after_grad), "ctx", compose, identity, True
    )[1]
    grad_trans = contract("hab,hdb->had", later_grad, incoming)
    grad_chain = chain_back((grad_block_trans, grad_block_seeds, grad_trans, later_grad))[0]
    grad_pieces = jax.tree.map(add_pair, grad_pieces_out, grad_chain)
    gradients = pieces_back(grad_pieces)
    arriving = from_behind((gradients[5], gradients[6], gradients[7]), "ctx", -1)

    def with_tail(grad_rows, tail_part):
        return grad_rows + jnp.pad(tail_part, ((rows_here - conv_lag, 0), (0, 0)))

    full_grads = (
        with_tail(gradients[0], arriving[0]),
        with_tail(gradients[1], arriving[1]),
        with_tail(gradients[2], arriving[2]),
        gradients[3],
        gradients[4],
    )
    partial_value = jnp.zeros((rows_here, query_weight.shape[0]), jnp.float32)
    for grad_rows, weight in zip(full_grads, weights):
        partial_value = partial_value + lax.dot_general(
            grad_rows.astype(jnp.bfloat16),
            weight,
            (((1,), (1,)), ((), ())),
            preferred_element_type=jnp.float32,
        )
    summed = lax.psum(partial_value.astype(jnp.bfloat16), "tp").astype(jnp.float32)
    share_width = summed.shape[1] // lax.axis_size("tp")
    own_share = lax.dynamic_slice_in_dim(summed, lax.axis_index("tp") * share_width, share_width, 1)
    return own_share.astype(jnp.bfloat16)


def solution(mesh):
    return jax.shard_map(
        local,
        mesh=mesh,
        in_specs=(
            P("ctx", "tp"),
            P(None, "tp"),
            P(None, "tp"),
            P(None, "tp"),
            P(None, "tp"),
            P(None, "tp"),
            P(None, "tp"),
            P(None, "tp"),
            P(None, "tp"),
            P("tp"),
            P("tp"),
            P("ctx", "tp"),
        ),
        out_specs=P("ctx", "tp"),
        check_vma=False,
    )
```

profile of v0, /device:TPU:0, one launch (start us, length us, event | category | flops | bytes accessed | tf_op | source)
XLA Modules:
  0.0 737.2 jit_solution(2436688149460652818)
XLA Ops:
  6.5 2.6 all_gather.27
  11.7 2.7 convolution_convert_fusion.2
  15.2 4.8 collective-permute-start
  20.5 4.0 collective-permute-start.1
  47.1 2.6 fusion.115
  57.5 3.1 convolution_subtract_fusion
  63.3 3.0 fusion.121
  69.4 12.3 %while.66 = (s32[]{:T(128)}, f32[8,128,128]{2,1,0:T(8,128)}, f32[8,128,128]{2,1,0:T(8,128)}, f32[2,8,128,128]{3,2,1,0:T(8,128)}, f32[2,8,128,128]{3,2,1,0:T(8,12...) while((s32[]{:T(128)}, f32[8,128,128]{2,1,0:T(8,128)}, ...), condition=%wide.region_3.4_spmd.clone, body=%wide.region_2.3_spmd.clone.sunk | while | flops 403046400 | bytes 12060307 | solution.py:165
  85.3 3.4 collective-permute-start.2
  91.7 2.4 fusion.159
  100.4 2.5 copy.395
  103.0 91.5 %all-gather.11.cloned.1.call-done = f32[128,128,128]{2,1,0:T(8,128)} async-done(((f32[8,128,128]{2,1,0:T(8,128)}), f32[128,128,128]{2,1,0:T(8,128)}) %all-gather.11.cloned.1.call-update) | async-done | bytes 8388624 | tf_op jit(solution)/shard_map/all_gather | solution.py:22
  194.4 113.8 %all-gather.9.cloned.1.call-done = f32[128,128,128]{2,1,0:T(8,128)} async-done(((f32[8,128,128]{2,1,0:T(8,128)}), f32[128,128,128]{2,1,0:T(8,128)}) %all-gather.9.cloned.1.call-update) | async-done | bytes 8388624 | tf_op jit(solution)/shard_map/all_gather | solution.py:22
  308.3 56.2 %while.67 = (s32[]{:T(128)}, f32[8,128,128]{2,1,0:T(8,128)}, s32[]{:T(128)}, f32[16,8,128,128]{3,2,1,0:T(8,128)}, f32[16,8,128,128]{3,2,1,0:T(8,128)}, /*index=5*/s32[]{:T(128)}, s32[]{:T(128)}) while((s32[]{:T(128)}, f32[8,128,128]{2,1,0:T(8,128)}, s32[]{:T(128)}, f32[16,8,128,128]{3,2,1,0:T(8,128)}, ...), condition=%wide.region_5.6_spmd.clone, body=%wide.region_4.5_spmd.clone.sunk | while | flops 201850880 | bytes 3672679 | solution.py:34
  309.7 2.7 fusion.393
  313.4 2.7 fusion.393
  317.1 2.7 fusion.393
  320.9 2.7 fusion.393
  324.6 2.7 fusion.393
  328.3 2.7 fusion.393
  332.0 2.7 fusion.393
  335.7 2.7 fusion.393
  339.5 2.7 fusion.393
  343.2 2.7 fusion.393
  346.9 2.7 fusion.393
  350.6 2.7 fusion.393
  354.3 2.7 fusion.393
  358.0 2.7 fusion.393
  361.7 2.7 fusion.393
  364.4 2.8 fusion.45
  367.2 3.7 convolution_subtract_fusion.1
  376.0 2.6 multiply_bitcast_fusion.2
  385.7 2.7 convolution_bitcast_fusion.2
  388.6 33.4 %all-gather.13.cloned.1.call-done = f32[128,128,128]{2,1,0:T(8,128)} async-done(((f32[8,128,128]{2,1,0:T(8,128)}), f32[128,128,128]{2,1,0:T(8,128)}) %all-gather.13.cloned.1.call-update) | async-done | bytes 8388624 | tf_op jit(solution)/shard_map/all_gather | solution.py:22
  422.1 7.9 %rev.6 = f32[16,8,128,128]{3,2,1,0:T(8,128)} reverse(f32[16,8,128,128]{3,2,1,0:T(8,128)} %bitcast.424), dimensions={0} | reverse | bytes 16777216 | tf_op jit(solution)/shard_map/rev | solution.py:24
  443.3 92.5 %all-gather.15.cloned.1.call-done = f32[128,128,128]{2,1,0:T(8,128)} async-done(((f32[8,128,128]{2,1,0:T(8,128)}), f32[128,128,128]{2,1,0:T(8,128)}) %all-gather.15.cloned.1.call-update) | async-done | bytes 8388624 | tf_op jit(solution)/shard_map/all_gather | solution.py:22
  535.8 7.8 %rev.7 = f32[16,8,128,128]{3,2,1,0:T(8,128)} reverse(f32[16,8,128,128]{3,2,1,0:T(8,128)} %bitcast.425), dimensions={0} | reverse | bytes 16777216 | tf_op jit(solution)/shard_map/rev | solution.py:24
  543.6 55.6 %while.68 = (s32[]{:T(128)}, f32[8,128,128]{2,1,0:T(8,128)}, s32[]{:T(128)}, f32[16,8,128,128]{3,2,1,0:T(8,128)}, f32[16,8,128,128]{3,2,1,0:T(8,128)}, /*index=5*/s32[]{:T(128)}, s32[]{:T(128)}) while((s32[]{:T(128)}, f32[8,128,128]{2,1,0:T(8,128)}, s32[]{:T(128)}, f32[16,8,128,128]{3,2,1,0:T(8,128)}, ...), condition=%wide.region_10.11_spmd.clone, body=%wide.region_9.10_spmd.clone.sunk | while | flops 201850880 | bytes 3672679 | solution.py:34
  544.6 2.7 fusion.396
  548.3 2.7 fusion.396
  552.0 2.7 fusion.396
  555.7 2.7 fusion.396
  559.4 2.7 fusion.396
  563.1 2.7 fusion.396
  566.8 2.7 fusion.396
  570.5 2.7 fusion.396
  574.3 2.7 fusion.396
  578.0 2.7 fusion.396
  581.7 2.7 fusion.396
  585.4 2.7 fusion.396
  589.1 2.7 fusion.396
  592.8 2.7 fusion.396
  596.5 2.7 fusion.396
  599.1 3.2 fusion.256
  604.5 22.9 %while.65 = (s32[]{:T(128)}, f32[8,128,128]{2,1,0:T(8,128)}, f32[8,128,128]{2,1,0:T(8,128)}, f32[2,8,128,128]{2,3,1,0:T(8,128)}, f32[2,8,128,128]{3,2,1,0:T(8,12...) while((s32[]{:T(128)}, f32[8,128,128]{2,1,0:T(8,128)}, ...), condition=%wide.region_12.13_spmd, body=%wide.region_11.12_spmd.sunk | while | flops 805699584 | bytes 27790576 | solution.py:165
  609.1 3.1 fusion.385
  620.5 3.1 fusion.385
  627.5 2.7 convolution_add_fusion.9
  630.2 4.4 fusion.257
  645.9 2.6 copy.446
  671.0 2.3 multiply_select_fusion
  698.5 3.2 collective-permute-done.5
  701.7 3.9 fusion.145
  708.5 20.3 %all-reduce.19.cloned.1.call-done = bf16[128,2048]{1,0:T(8,128)(2,1)} async-done(((bf16[128,2048]{1,0:T(8,128)(2,1)}), bf16[128,2048]{1,0:T(8,128)(2,1)}) %all-reduce.19.cloned.1.call-update) | async-done | bytes 524304 | tf_op jit(solution)/shard_map/psum | solution.py:285
  (466 shorter events, 202.9 us)
Async XLA Ops:
  6.5 187.9 %all-gather.11.cloned.1.call-start = ((), (), s32[]{:S(2)}) async-start(), calls=%async_computation.2 | async-start | bytes 8912896 | tf_op jit(solution)/shard_map/all_gather | solution.py:22
  6.5 7.8 %copy-start.19 = (bf16[2048,1024]{1,0:T(8,128)(2,1)S(1)}, bf16[2048,1024]{1,0:T(8,128)(2,1)}, u32[]{:S(2)}) copy-start(bf16[2048,1024]{1,0:T(8,128)(2,1)} %param.23) | copy-start | bytes 12582916
  10.1 15.1 %copy-start.96 = (bf16[128,8]{0,1:T(8,128)(2,1)}, bf16[128,8]{0,1:T(8,128)(2,1)S(1)}, u32[]{:S(2)}) copy-start(bf16[128,8]{0,1:T(8,128)(2,1)S(1)} %convolution_convert_fusion.3) | copy-start | bytes 6148
  11.1 14.1 %copy-start.98 = (bf16[128,8]{0,1:T(8,128)(2,1)}, bf16[128,8]{0,1:T(8,128)(2,1)S(1)}, u32[]{:S(2)}) copy-start(bf16[128,8]{0,1:T(8,128)(2,1)S(1)} %convolution_convert_fusion.4) | copy-start | bytes 6148
  11.6 12.9 %copy-start.117 = (f32[8]{0:T(128)S(1)}, f32[8]{0:T(128)}, u32[]{:S(2)}) copy-start(f32[8]{0:T(128)} %param.29) | copy-start | bytes 100
  11.6 12.9 %copy-start.110 = (bf16[4,512]{1,0:T(4,128)(2,1)S(1)}, bf16[4,512]{1,0:T(4,128)(2,1)}, u32[]{:S(2)}) copy-start(bf16[4,512]{1,0:T(4,128)(2,1)} %param.27) | copy-start | bytes 12292
  11.6 13.0 %copy-start.92 = (bf16[4,1024]{1,0:T(4,128)(2,1)S(1)}, bf16[4,1024]{1,0:T(4,128)(2,1)}, u32[]{:S(2)}) copy-start(bf16[4,1024]{1,0:T(4,128)(2,1)} %param.28) | copy-start | bytes 24580
  11.7 13.6 %copy-start.113 = (f32[8]{0:T(128)S(1)}, f32[8]{0:T(128)}, u32[]{:S(2)}) copy-start(f32[8]{0:T(128)} %param.30) | copy-start | bytes 100
  15.2 13.1 %collective-permute-start = (bf16[3,512]{1,0:T(4,128)(2,1)S(1)}, bf16[3,512]{1,0:T(4,128)(2,1)S(1)}, u32[]{:S(2)}, u32[]{:S(2)}) collective-permute-start(bf16[3,512]{1,0:T(4,128)(2,1)S(1)} %slice.78), channel_id=1, source_target_pairs={{0,2},{2,4},{4,6},{6,8},{8,10},{10,12},{12,14},{14,16},{16,18},{18... | collective-permute-start | bytes 9224 | tf_op jit(solution)/shard_map/ppermute | solution.py:17
  20.5 40.1 %collective-permute-start.1 = (bf16[3,1024]{1,0:T(4,128)(2,1)}, bf16[3,1024]{1,0:T(4,128)(2,1)}, u32[]{:S(2)}, u32[]{:S(2)}) collective-permute-start(bf16[3,1024]{1,0:T(4,128)(2,1)} %slice.86), channel_id=1, source_target_pairs={{0,2},{2,4},{4,6},{6,8},{8,10},{10,12},{12,14},{14,16},{16,18},{18... | collective-permute-start | bytes 18440 | tf_op jit(solution)/shard_map/ppermute | solution.py:17
  28.5 9.1 %copy-start.64 = (f32[128,512]{1,0:T(8,128)}, f32[128,512]{1,0:T(8,128)S(1)}, u32[]{:S(2)}) copy-start(f32[128,512]{1,0:T(8,128)S(1)} %get-tuple-element.639) | copy-start | bytes 786436
  30.0 25.7 %copy-start.1 = (f32[128,4,2,128]{3,0,2,1:T(8,128)}, f32[128,4,2,128]{3,0,2,1:T(8,128)S(1)}, u32[]{:S(2)}) copy-start(f32[128,4,2,128]{3,0,2,1:T(8,128)S(1)} %broadcast_in_dim.103) | copy-start | bytes 1572868
  34.6 12.4 %copy-start.10 = (f32[2,8,64,64]{3,2,1,0:T(8,128)}, f32[2,8,64,64]{3,2,1,0:T(8,128)S(1)}, u32[]{:S(2)}) copy-start(f32[2,8,64,64]{3,2,1,0:T(8,128)S(1)} %fusion.252) | copy-start | bytes 786436
  44.7 8.0 %copy-start.49 = (f32[2,8,64,64]{2,3,1,0:T(8,128)S(1)}, f32[2,8,64,64]{2,3,1,0:T(8,128)}, u32[]{:S(2)}) copy-start(f32[2,8,64,64]{2,3,1,0:T(8,128)} %copy.386) | copy-start | bytes 786436
  44.7 9.0 %copy-start.50 = (f32[2,8,64,64]{2,3,1,0:T(8,128)S(1)}, f32[2,8,64,64]{2,3,1,0:T(8,128)}, u32[]{:S(2)}) copy-start(f32[2,8,64,64]{2,3,1,0:T(8,128)} %copy.388) | copy-start | bytes 786436
  47.0 8.6 %copy-start.44 = (f32[2,8,64,64]{2,3,1,0:T(8,128)}, f32[2,8,64,64]{2,3,1,0:T(8,128)S(1)}, u32[]{:S(2)}) copy-start(f32[2,8,64,64]{2,3,1,0:T(8,128)S(1)} %convolution_add_fusion.22) | copy-start | bytes 786436
  47.1 8.7 %copy-start.76 = (f32[2,8,64]{2,1,0:T(8,128)S(1)}, f32[2,8,64]{2,1,0:T(8,128)}, u32[]{:S(2)}) copy-start(f32[2,8,64]{2,1,0:T(8,128)} %get-tuple-element.659) | copy-start | bytes 12292
  49.7 10.9 %copy-start.51 = (f32[2,8,64,64]{3,2,1,0:T(8,128)}, f32[2,8,64,64]{3,2,1,0:T(8,128)S(1)}, u32[]{:S(2)}) copy-start(f32[2,8,64,64]{3,2,1,0:T(8,128)S(1)} %fusion.115) | copy-start | bytes 786436
  49.7 7.8 %copy-start.112 = (f32[2,8]{1,0:T(2,128)S(1)}, f32[2,8]{1,0:T(2,128)}, u32[]{:S(2)}) copy-start(f32[2,8]{1,0:T(2,128)} %exp.69) | copy-start | bytes 196
  52.7 8.6 %copy-start.69 = (f32[128,1024]{1,0:T(8,128)S(1)}, f32[128,1024]{1,0:T(8,128)}, u32[]{:S(2)}) copy-start(f32[128,1024]{1,0:T(8,128)} %convert_element_type.133) | copy-start | bytes 1572868
  52.7 8.6 %copy-start.81 = (f32[1,1024]{1,0:T(1,128)S(1)}, f32[1,1024]{1,0:T(1,128)}, u32[]{:S(2)}) copy-start(f32[1,1024]{1,0:T(1,128)} %get-tuple-element.665) | copy-start | bytes 12292
  52.7 8.6 %copy-start.83 = (f32[1,1024]{1,0:T(1,128)S(1)}, f32[1,1024]{1,0:T(1,128)}, u32[]{:S(2)}) copy-start(f32[1,1024]{1,0:T(1,128)} %get-tuple-element.666) | copy-start | bytes 12292
  52.7 8.6 %copy-start.85 = (f32[1,1024]{1,0:T(1,128)S(1)}, f32[1,1024]{1,0:T(1,128)}, u32[]{:S(2)}) copy-start(f32[1,1024]{1,0:T(1,128)} %get-tuple-element.668) | copy-start | bytes 12292
  52.7 8.6 %copy-start.87 = (f32[1,1024]{1,0:T(1,128)S(1)}, f32[1,1024]{1,0:T(1,128)}, u32[]{:S(2)}) copy-start(f32[1,1024]{1,0:T(1,128)} %get-tuple-element.667) | copy-start | bytes 12292
  55.7 10.6 %copy-start.20 = (f32[2,8,64,64]{3,2,1,0:T(8,128)}, f32[2,8,64,64]{3,2,1,0:T(8,128)S(1)}, u32[]{:S(2)}) copy-start(f32[2,8,64,64]{3,2,1,0:T(8,128)S(1)} %fusion.255) | copy-start | bytes 786436
  69.4 15.3 %copy-start.73 = (bf16[128,512]{1,0:T(8,128)(2,1)S(1)}, bf16[128,512]{1,0:T(8,128)(2,1)}, u32[]{:S(2)}) copy-start(bf16[128,512]{1,0:T(8,128)(2,1)} %convolution_convert_fusion.2) | copy-start | bytes 393220
  69.4 19.3 %copy-start.111 = (bf16[4,512]{1,0:T(4,128)(2,1)S(1)}, bf16[4,512]{1,0:T(4,128)(2,1)}, u32[]{:S(2)}) copy-start(bf16[4,512]{1,0:T(4,128)(2,1)} %param.26) | copy-start | bytes 12292
  81.7 226.5 %all-gather.9.cloned.1.call-start = ((), (), s32[]{:S(2)}) async-start(), calls=%async_computation.1 | async-start | bytes 8912896 | tf_op jit(solution)/shard_map/all_gather | solution.py:22
  82.5 339.6 %all-gather.13.cloned.1.call-start = ((), (), s32[]{:S(2)}) async-start(), calls=%async_computation.3 | async-start | bytes 8912896 | tf_op jit(solution)/shard_map/all_gather | solution.py:22
  84.6 451.1 %all-gather.15.cloned.1.call-start = ((), (), s32[]{:S(2)}) async-start(), calls=%async_computation.4 | async-start | bytes 8912896 | tf_op jit(solution)/shard_map/all_gather | solution.py:22
  85.3 5.7 collective-permute-start.2
  364.4 7.7 %copy-start.3 = (f32[128,4,2,128]{3,0,2,1:T(8,128)S(1)}, f32[128,4,2,128]{3,0,2,1:T(8,128)}, u32[]{:S(2)}) copy-start(f32[128,4,2,128]{3,0,2,1:T(8,128)} %copy-done.1) | copy-start | bytes 1572868
  364.4 7.7 %copy-start.90 = (f32[2,64,8]{1,2,0:T(8,128)S(1)}, f32[2,64,8]{1,2,0:T(8,128)}, u32[]{:S(2)}) copy-start(f32[2,64,8]{1,2,0:T(8,128)} %get-tuple-element.658) | copy-start | bytes 12292
  388.4 340.4 %all-reduce.19.cloned.1.call-start = ((), (), s32[]{:S(2)}) async-start(), calls=%async_computation | async-start | bytes 1048576 | tf_op jit(solution)/shard_map/psum | solution.py:285
  422.1 11.8 %copy-start.68 = (f32[128,512]{1,0:T(8,128)S(1)}, f32[128,512]{1,0:T(8,128)}, u32[]{:S(2)}) copy-start(f32[128,512]{1,0:T(8,128)} %get-tuple-element.635) | copy-start | bytes 786436
  432.6 8.6 %copy-start.5 = (f32[8,128,128]{2,1,0:T(8,128)S(1)}, f32[8,128,128]{2,1,0:T(8,128)}, u32[]{:S(2)}) copy-start(f32[8,128,128]{2,1,0:T(8,128)} %get-tuple-element.443) | copy-start | bytes 1572868
  432.6 8.6 %copy-start.7 = (f32[2,8,128,128]{3,2,1,0:T(8,128)S(1)}, f32[2,8,128,128]{3,2,1,0:T(8,128)}, u32[]{:S(2)}) copy-start(f32[2,8,128,128]{3,2,1,0:T(8,128)} %copy-done.6) | copy-start | bytes 3145732
  436.4 269.2 %collective-permute-start.3 = (f32[3,512]{1,0:T(4,128)}, f32[3,512]{1,0:T(4,128)}, u32[]{:S(2)}, u32[]{:S(2)}) collective-permute-start(f32[3,512]{1,0:T(4,128)} %pad_add_fusion.5), channel_id=1, source_target_pairs={{2,0},{4,2},{6,4},{8,6},{10,8},{12,10},{14,12},{16,14},{18,16},{20... | collective-permute-start | bytes 18440 | tf_op jit(solution)/shard_map/ppermute | solution.py:17
  604.5 7.7 %copy-start.32 = (f32[2,8,128,128]{3,2,0,1:T(8,128)S(1)}, f32[2,8,128,128]{3,2,0,1:T(8,128)}, u32[]{:S(2)}) copy-start(f32[2,8,128,128]{3,2,0,1:T(8,128)} %get-tuple-element.953) | copy-start | bytes 3145732 | tf_op jit(solution)/shard_map/transpose(jvp())/while
  604.5 9.5 %copy-start.34 = (f32[2,8,128,128]{3,2,1,0:T(8,128)S(1)}, f32[2,8,128,128]{3,2,1,0:T(8,128)}, u32[]{:S(2)}) copy-start(f32[2,8,128,128]{3,2,1,0:T(8,128)} %get-tuple-element.941) | copy-start | bytes 3145732 | tf_op jit(solution)/shard_map/transpose(jvp())/while
  605.7 8.3 %copy-start.8 = (f32[2,8,128,128]{3,2,1,0:T(8,128)S(1)}, f32[2,8,128,128]{3,2,1,0:T(8,128)}, u32[]{:S(2)}) copy-start(f32[2,8,128,128]{3,2,1,0:T(8,128)} %get-tuple-element.955) | copy-start | bytes 3145732 | tf_op jit(solution)/shard_map/transpose(jvp())/while
  615.9 7.6 %copy-start.32 = (f32[2,8,128,128]{3,2,0,1:T(8,128)S(1)}, f32[2,8,128,128]{3,2,0,1:T(8,128)}, u32[]{:S(2)}) copy-start(f32[2,8,128,128]{3,2,0,1:T(8,128)} %get-tuple-element.953) | copy-start | bytes 3145732 | tf_op jit(solution)/shard_map/transpose(jvp())/while
  615.9 9.5 %copy-start.34 = (f32[2,8,128,128]{3,2,1,0:T(8,128)S(1)}, f32[2,8,128,128]{3,2,1,0:T(8,128)}, u32[]{:S(2)}) copy-start(f32[2,8,128,128]{3,2,1,0:T(8,128)} %get-tuple-element.941) | copy-start | bytes 3145732 | tf_op jit(solution)/shard_map/transpose(jvp())/while
  617.1 8.3 %copy-start.8 = (f32[2,8,128,128]{3,2,1,0:T(8,128)S(1)}, f32[2,8,128,128]{3,2,1,0:T(8,128)}, u32[]{:S(2)}) copy-start(f32[2,8,128,128]{3,2,1,0:T(8,128)} %get-tuple-element.955) | copy-start | bytes 3145732 | tf_op jit(solution)/shard_map/transpose(jvp())/while
  627.4 7.2 copy-start.4
  627.4 7.2 copy-start.17
  627.5 7.2 copy-start.70
  627.5 9.3 %copy-start.77 = (f32[2,8,64]{2,1,0:T(8,128)S(1)}, f32[2,8,64]{2,1,0:T(8,128)}, u32[]{:S(2)}) copy-start(f32[2,8,64]{2,1,0:T(8,128)} %get-tuple-element.659) | copy-start | bytes 12292
  627.5 10.4 %copy-start.21 = (f32[2,8,64,64]{3,2,1,0:T(8,128)S(1)}, f32[2,8,64,64]{3,2,1,0:T(8,128)}, u32[]{:S(2)}) copy-start(f32[2,8,64,64]{3,2,1,0:T(8,128)} %copy-done.20) | copy-start | bytes 786436
  630.2 9.5 %copy-start.38 = (f32[16,8,8,128]{3,2,1,0:T(8,128)S(1)}, f32[16,8,8,128]{3,2,1,0:T(8,128)}, u32[]{:S(2)}) copy-start(f32[16,8,8,128]{3,2,1,0:T(8,128)} %copy-done.37) | copy-start | bytes 1572868
  636.8 7.3 copy-start.47
  645.9 9.6 %copy-start.14 = (f32[2,8,64,64]{3,2,1,0:T(8,128)S(1)}, f32[2,8,64,64]{3,2,1,0:T(8,128)}, u32[]{:S(2)}) copy-start(f32[2,8,64,64]{3,2,1,0:T(8,128)} %fusion.254) | copy-start | bytes 786436
  673.9 7.6 %copy-start.109 = (f32[128,4]{0,1:T(4,128)S(1)}, f32[128,4]{0,1:T(4,128)}, u32[]{:S(2)}) copy-start(f32[128,4]{0,1:T(4,128)} %copy-done.108) | copy-start | bytes 6148
  674.9 8.3 %copy-start.107 = (f32[1,512]{1,0:T(1,128)S(1)}, f32[1,512]{1,0:T(1,128)}, u32[]{:S(2)}) copy-start(f32[1,512]{1,0:T(1,128)} %copy-done.106) | copy-start | bytes 6148
  674.9 9.5 %copy-start.101 = (f32[1,512]{1,0:T(1,128)S(1)}, f32[1,512]{1,0:T(1,128)}, u32[]{:S(2)}) copy-start(f32[1,512]{1,0:T(1,128)} %copy-done.100) | copy-start | bytes 6148
  674.9 9.5 %copy-start.103 = (f32[1,512]{1,0:T(1,128)S(1)}, f32[1,512]{1,0:T(1,128)}, u32[]{:S(2)}) copy-start(f32[1,512]{1,0:T(1,128)} %copy-done.102) | copy-start | bytes 6148
  674.9 9.5 %copy-start.105 = (f32[1,512]{1,0:T(1,128)S(1)}, f32[1,512]{1,0:T(1,128)}, u32[]{:S(2)}) copy-start(f32[1,512]{1,0:T(1,128)} %copy-done.104) | copy-start | bytes 6148
  677.0 8.4 %copy-start.67 = (f32[2,8,128,128]{3,2,1,0:T(8,128)S(1)}, f32[2,8,128,128]{3,2,1,0:T(8,128)}, u32[]{:S(2)}) copy-start(f32[2,8,128,128]{3,2,1,0:T(8,128)} %copy.446) | copy-start | bytes 3145732
  677.8 7.8 %copy-start.78 = (f32[2,8,64]{2,1,0:T(8,128)S(1)}, f32[2,8,64]{2,1,0:T(8,128)}, u32[]{:S(2)}) copy-start(f32[2,8,64]{2,1,0:T(8,128)} %get-tuple-element.570) | copy-start | bytes 12292
  688.9 7.8 %collective-permute-start.4 = (f32[3,512]{1,0:T(4,128)S(1)}, f32[3,512]{1,0:T(4,128)S(1)}, u32[]{:S(2)}, u32[]{:S(2)}) collective-permute-start(f32[3,512]{1,0:T(4,128)S(1)} %pad_add_fusion.4), channel_id=1, source_target_pairs={{2,0},{4,2},{6,4},{8,6},{10,8},{12,10},{14,12},{16,14},{18,16},{20... | collective-permute-start | bytes 18440 | tf_op jit(solution)/shard_map/ppermute | solution.py:17
  695.1 10.4 %copy-start.36 = (bf16[2048,512]{1,0:T(8,128)(2,1)S(1)}, bf16[2048,512]{1,0:T(8,128)(2,1)}, u32[]{:S(2)}) copy-start(bf16[2048,512]{1,0:T(8,128)(2,1)} %param.21) | copy-start | bytes 6291460
  695.1 10.5 %copy-start.66 = (f32[128,2048]{1,0:T(8,128)S(1)}, f32[128,2048]{1,0:T(8,128)}, u32[]{:S(2)}) copy-start(f32[128,2048]{1,0:T(8,128)} %fusion.222) | copy-start | bytes 3145732
  695.1 10.5 %copy-start.72 = (f32[131,512]{1,0:T(8,128)S(1)}, f32[131,512]{1,0:T(8,128)}, u32[]{:S(2)}) copy-start(f32[131,512]{1,0:T(8,128)} %pad_add_fusion.2) | copy-start | bytes 804868
  695.1 6.5 collective-permute-start.5
  (70 other events, 295.8 us)
Sparse Core Ops, SparseCore 0:
  81.8 112.5 all-gather.10
  197.2 111.0 all-gather.8
  311.0 111.0 all-gather.12
  424.7 111.0 all-gather.14
  708.6 20.1 all-reduce.18
where the time goes:
time: 751 us; the launch traced here: 737 us
  waiting for transfers between devices  355 us (47%)
  matrix products  212 us (28%)
  local copies, waits for them, and re-layouts  95.6 us (13%)
  other arithmetic  38.8 us (5%)
  starting transfers between devices  16.6 us (2%)
  between operations  15.1 us (2%)
    all_gather x4, waiting for transfers between devices, entering(): pieces = jax.tree.map(lambda part: lax.all_gather(part, axis), value)  331 us
    dot_general x101, matrix products, contract(): jnp.einsum(form, left_arr, right_arr, precision=lax.Precision.HIGHEST, pr...  197 us
    while x58, local copies, waits for them, and re-layouts  40.4 us
    psum x1, waiting for transfers between devices, local(): lax.psum(partial_value.astype(jnp.bfloat16), 'tp').astype(jnp.float32)  20.3 us
    ppermute x6, starting transfers between devices, from_behind(): lax.ppermute(value, axis, [(source, source + steps) for source in range(l...  16.3 us
    rev x2, local copies, waits for them, and re-layouts, entering(): pieces = jax.tree.map(lambda part: part[::-1], pieces)  15.7 us
  transfers between devices with their start and end apart: 11, of which 6 were waited for; matrix products, arithmetic and copies ran while one was open for 42% of the time, Pallas kernels for 0%

commit v1 on v0

v1 whole, which is shorter than its diff:
```python
import functools

import jax
import jax.numpy as jnp
from jax import lax
from jax.experimental import pallas as pl
from jax.experimental.pallas import tpu as pltpu
from jax.sharding import PartitionSpec as P

DH = 128
CONV = 4
EPS = 1e-06
MESH = pl.DeviceIdType.MESH
BF = jnp.bfloat16
F32 = jnp.float32


def mm(left, right, lc, rc):
    return lax.dot_general(
        left.astype(BF), right.astype(BF), (((lc,), (rc,)), ((), ())), preferred_element_type=F32
    )


def nn(left, right):
    return mm(left, right, 1, 0)


def nt(left, right):
    return mm(left, right, 1, 1)


def tn(left, right):
    return mm(left, right, 0, 0)


def rowsum(value):
    return jnp.sum(value, axis=1, keepdims=True)


def colsum(value):
    return jnp.sum(value, axis=0, keepdims=True)


def column(ref, head):
    value = ref[...]
    lanes = lax.broadcasted_iota(jnp.int32, value.shape, 1)
    return rowsum(jnp.where(lanes == head, value, 0.0))


def lane_block(head):
    return pl.ds(pl.multiple_of(head * DH, DH), DH)


def inverses(stricts):
    size = stricts[0].shape[0]
    row = lax.broadcasted_iota(jnp.int32, (size, size), 0)
    col = lax.broadcasted_iota(jnp.int32, (size, size), 1)
    results = [jnp.where(row == col, 1.0, 0.0) - jnp.where((row // 2) == (col // 2), a, 0.0) for a in stricts]
    block = 2
    while block < size:
        within = ((row // (2 * block)) == (col // (2 * block))) & ((row // block) > (col // block))
        parts = [jnp.where(within, a, 0.0) for a in stricts]
        halves = [nn(a, m) for a, m in zip(parts, results)]
        results = [m - nn(m, a) for m, a in zip(results, halves)]
        block *= 2
    return results


def core_kernel(
    kheads, ratio, group,
    q_ref, k_ref, v_ref, beta_ref, gc_ref, gr_ref, do_ref,
    dq_ref, dk_ref, dv_ref, dbeta_ref, dgc_ref, dgr_ref,
    inv_s, w_s, vm_s, y_s, move_s, add_s, end_s, land_s, out_s,
    send_sem, recv_sem,
):
    count, me = lax.axis_size("ctx"), lax.axis_index("ctx")
    vheads = kheads * ratio
    size = q_ref.shape[0]
    row = lax.broadcasted_iota(jnp.int32, (size, size), 0)
    col = lax.broadcasted_iota(jnp.int32, (size, size), 1)
    lower, strictly = row >= col, row > col

    barrier = pltpu.get_barrier_semaphore()

    @pl.when(me > 0)
    def _():
        pl.semaphore_signal(barrier, inc=1, device_id={"ctx": me - 1}, device_id_type=MESH)

    @pl.when(me < count - 1)
    def _():
        pl.semaphore_signal(barrier, inc=1, device_id={"ctx": me + 1}, device_id_type=MESH)

    def gates(head):
        gc, gr = column(gc_ref, head), gr_ref[pl.ds(head, 1), :]
        decay = jnp.where(lower, jnp.exp(jnp.where(lower, gc - gr, 0.0)), 0.0)
        last = gc[size - 1 : size, :]
        return column(beta_ref, head), decay, jnp.exp(gc), jnp.exp(last - gc), jnp.exp(last)

    def prepare(step, carry):
        kh = [step * group + i for i in range(group)]
        ks = [k_ref[:, lane_block(h)] for h in kh]
        qs = [q_ref[:, lane_block(h)] for h in kh]
        kk = [nt(k, k) for k in ks]
        qk = [nt(q, k) for q, k in zip(qs, ks)]
        heads = [(i, kh[i] * ratio + r) for i in range(group) for r in range(ratio)]
        gate = [gates(h) for _, h in heads]
        stricts = [
            jnp.where(strictly, g[0] * kk[i] * g[1], 0.0) for (i, _), g in zip(heads, gate)
        ]
        invs = inverses(stricts)
        dos = [do_ref[:, lane_block(h)] for _, h in heads]
        ys = [tn(qk[i] * g[1], do) for (i, _), g, do in zip(heads, gate, dos)]
        ws = [nn(m, (g[0] * g[2]) * ks[i]) for (i, _), g, m in zip(heads, gate, invs)]
        vms = [nn(m, g[0] * v_ref[:, lane_block(h)]) for (_, h), g, m in zip(heads, gate, invs)]
        kts = [g[3] * ks[i] for (i, _), g in zip(heads, gate)]
        for n, (i, h) in enumerate(heads):
            inv_s[h] = invs[n].astype(BF)
            w_s[h] = ws[n].astype(BF)
            vm_s[h] = vms[n]
            y_s[h] = ys[n]
            end_s[h] = jnp.broadcast_to(gate[n][4], (8, DH))
            move_s[0, h] = tn(kts[n], ws[n]).astype(BF)
            move_s[1, h] = tn(ws[n], kts[n]).astype(BF)
            add_s[0, h] = tn(kts[n], vms[n])
            add_s[1, h] = tn(gate[n][2] * qs[i], dos[n]) - tn(ws[n], ys[n])
        return carry

    lax.fori_loop(0, kheads // group, prepare, 0)

    peers = jnp.minimum(me, 1) + jnp.minimum(count - 1 - me, 1)
    pl.semaphore_wait(barrier, peers)

    @pl.when(me == 0)
    def _():
        land_s[0] = jnp.zeros(land_s.shape[1:], land_s.dtype)

    @pl.when(me == count - 1)
    def _():
        land_s[1] = jnp.zeros(land_s.shape[1:], land_s.dtype)

    late = (2 * me) // count

    def hop(way, head, target):
        return pltpu.make_async_remote_copy(
            src_ref=out_s.at[way, head],
            dst_ref=land_s.at[way, head],
            send_sem=send_sem.at[way, head],
            recv_sem=recv_sem.at[way, head],
            device_id={"ctx": target},
            device_id_type=MESH,
        )

    def chain(step, carry):
        turn, head = step // vheads, step % vheads
        way = turn + late - 2 * turn * late
        before, after = me - 1 + 2 * way, me + 1 - 2 * way

        @pl.when((before >= 0) & (before < count))
        def _():
            hop(way, head, before).wait_recv()

        @pl.when((after >= 0) & (after < count))
        def _():
            state = land_s[way, head]
            out_s[way, head] = (
                end_s[head][0:1, :] * state.astype(F32)
                - nn(move_s[way, head], state)
                + add_s[way, head]
            ).astype(BF)
            hop(way, head, after).start()

        return carry

    lax.fori_loop(0, 2 * vheads, chain, 0)

    dbeta_ref[...] = jnp.zeros(dbeta_ref.shape, F32)
    dgc_ref[...] = jnp.zeros(dgc_ref.shape, F32)
    gate_lanes = lax.broadcasted_iota(jnp.int32, dbeta_ref.shape, 1)
    at_end = lax.broadcasted_iota(jnp.int32, (size, 1), 0) == size - 1

    def back(step, carry):
        kh = [step * group + i for i in range(group)]
        ks = [k_ref[:, lane_block(h)] for h in kh]
        qs = [q_ref[:, lane_block(h)] for h in kh]
        kk = [nt(k, k) for k in ks]
        qk = [nt(q, k) for q, k in zip(qs, ks)]
        heads = [(i, kh[i] * ratio + r) for i in range(group) for r in range(ratio)]
        span = range(len(heads))
        gate = [gates(h) for _, h in heads]
        own_k = [ks[i] for i, _ in heads]
        own_q = [qs[i] for i, _ in heads]
        dos = [do_ref[:, lane_block(h)] for _, h in heads]
        vs = [v_ref[:, lane_block(h)] for _, h in heads]
        starts = [land_s[0, h] for _, h in heads]
        ends = [land_s[1, h] for _, h in heads]
        fresh = [vm_s[h] - nn(w_s[h], starts[n]) for n, (_, h) in enumerate(heads)]
        xs = [nn(own_k[n], starts[n]) for n in span]
        dfresh = [
            y_s[h] + nn(gate[n][3] * own_k[n], ends[n]) for n, (_, h) in enumerate(heads)
        ]
        drs = [tn(inv_s[h], dfresh[n]) for n, (_, h) in enumerate(heads)]
        dps = [nt(dos[n], fresh[n]) for n in span]
        dqs = [nt(dos[n], starts[n]) for n in span]
        dkt = [nt(fresh[n], ends[n]) for n in span]
        das = [jnp.where(strictly, -nt(drs[n], fresh[n]), 0.0) for n in span]
        dxs = [nt((gate[n][0] * gate[n][2]) * drs[n], starts[n]) for n in span]
        dqk = [0.0] * group
        dkk = [0.0] * group
        dq = [0.0] * group
        dk = [0.0] * group
        for n, (i, h) in enumerate(heads):
            beta, decay, gam, tail, end = gate[n]
            k, q = own_k[n], own_q[n]
            dpd = dps[n] * decay
            dad = das[n] * decay
            dad_kk = dad * kk[i]
            dqk[i] += dpd
            dkk[i] += beta * dad
            logs = dpd * qk[i] + beta * dad_kk
            dgam = rowsum(q * dqs[n]) - beta * rowsum(drs[n] * xs[n])
            dtail = rowsum(k * dkt[n]) * tail
            dend = jnp.sum(
                starts[n].astype(F32) * ends[n].astype(F32), axis=(0, 1), keepdims=True
            ) * end
            dbeta = rowsum(drs[n] * (vs[n] - gam * xs[n])) + rowsum(dad_kk)
            dgc = rowsum(logs) + dgam * gam - dtail
            dgc += jnp.where(at_end, colsum(dtail) + dend, 0.0)
            dq[i] += gam * dqs[n]
            dk[i] += tail * dkt[n] - dxs[n]
            dv_ref[:, lane_block(h)] = beta * drs[n]
            dbeta_ref[...] += jnp.where(gate_lanes == h, dbeta, 0.0)
            dgc_ref[...] += jnp.where(gate_lanes == h, dgc, 0.0)
            dgr_ref[pl.ds(h, 1), :] = -colsum(logs)
        for i in range(group):
            dq_ref[:, lane_block(kh[i])] = dq[i] + nn(dqk[i], ks[i])
            dk_ref[:, lane_block(kh[i])] = (
                dk[i] + tn(dqk[i], qs[i]) + nn(dkk[i], ks[i]) + tn(dkk[i], ks[i])
            )
        return carry

    lax.fori_loop(0, kheads // group, back, 0)

    def drain(head, carry):
        @pl.when(me < count - 1)
        def _():
            hop(0, head, me + 1).wait_send()

        @pl.when(me > 0)
        def _():
            hop(1, head, me - 1).wait_send()

        return carry

    lax.fori_loop(0, vheads, drain, 0)


def recurrence_grads(q, k, v, beta, gc, gr, grad_core):
    size = q.shape[0]
    kheads, vheads = q.shape[1] // DH, v.shape[1] // DH
    ratio = vheads // kheads
    group = 2 if kheads % 2 == 0 else 1
    shapes = [q, k, v, beta, gc, gr]
    square = (DH, DH)
    vmem = pl.BlockSpec(memory_space=pltpu.VMEM)
    return pl.pallas_call(
        functools.partial(core_kernel, kheads, ratio, group),
        out_shape=[jax.ShapeDtypeStruct(a.shape, F32) for a in shapes],
        in_specs=[vmem] * 7,
        out_specs=[vmem] * 6,
        scratch_shapes=[
            pltpu.VMEM((vheads, size, size), BF),
            pltpu.VMEM((vheads, size, DH), BF),
            pltpu.VMEM((vheads, size, DH), F32),
            pltpu.VMEM((vheads, size, DH), F32),
            pltpu.VMEM((2, vheads) + square, BF),
            pltpu.VMEM((2, vheads) + square, F32),
            pltpu.VMEM((vheads, 8, DH), F32),
            pltpu.VMEM((2, vheads) + square, BF),
            pltpu.VMEM((2, vheads) + square, BF),
            pltpu.SemaphoreType.DMA((2, vheads)),
            pltpu.SemaphoreType.DMA((2, vheads)),
        ],
        compiler_params=pltpu.CompilerParams(
            collective_id=0, has_side_effects=True, vmem_limit_bytes=40 * 1024 * 1024
        ),
    )(q, k, v, beta, gc, gr, grad_core)


def from_behind(value, axis, steps):
    count = lax.axis_size(axis)
    leading, last = (max(0, -steps), min(count, count - steps))
    return lax.ppermute(value, axis, [(source, source + steps) for source in range(leading, last)])


def conv_silu(padded, weight):
    tap_count = weight.shape[0]
    length = padded.shape[0] - tap_count + 1
    running = jnp.zeros((length, padded.shape[1]), F32)
    for tap in range(tap_count):
        running = running + weight[tap].astype(F32) * padded[tap : tap + length]
    return jax.nn.silu(running)


def normalized(rows_in, scale):
    shaped = rows_in.reshape(rows_in.shape[0], -1, DH)
    unit = shaped * (lax.rsqrt(jnp.sum(shaped * shaped, axis=-1, keepdims=True) + EPS) * scale)
    return unit.reshape(rows_in.shape)


def running_sum(log_decay):
    size = log_decay.shape[0]
    row = lax.broadcasted_iota(jnp.int32, (size, size), 0)
    col = lax.broadcasted_iota(jnp.int32, (size, size), 1)
    return jnp.dot(
        jnp.where(row >= col, 1.0, 0.0), log_decay, precision=lax.Precision.HIGHEST,
        preferred_element_type=F32,
    )


def local(
    inputs, query_weight, key_weight, value_weight, beta_weight, alpha_weight,
    query_filter, key_filter, value_filter, decay_log, step_bias, grad_core,
):
    rows_here = inputs.shape[0]
    lag = CONV - 1
    weights = (query_weight, key_weight, value_weight, beta_weight, alpha_weight)
    pair = lax.axis_size("tp") == 2
    side = lax.axis_index("tp")
    if pair:
        other = lax.ppermute(inputs, "tp", [(0, 1), (1, 0)])
        whole = jnp.where(
            side == 0,
            jnp.concatenate([inputs, other], 1),
            jnp.concatenate([other, inputs], 1),
        )
    else:
        whole = lax.all_gather(inputs, "tp", axis=1, tiled=True)
    rounded = lax.optimization_barrier(
        tuple(jnp.dot(whole, w, preferred_element_type=F32).astype(BF) for w in weights)
    )
    tails = from_behind(
        jnp.concatenate([m[rows_here - lag :] for m in rounded[:3]], 1), "ctx", 1
    )
    widths = [m.shape[1] for m in rounded[:3]]
    cuts = [0, widths[0], widths[0] + widths[1], sum(widths)]
    tails = [tails[:, cuts[n] : cuts[n + 1]] for n in range(3)]
    padded = [jnp.concatenate([t, m], 0).astype(F32) for t, m in zip(tails, rounded)]

    def front(query_pad, key_pad, value_pad, beta_raw, alpha_raw):
        q = normalized(conv_silu(query_pad, query_filter), DH ** (-0.5))
        k = normalized(conv_silu(key_pad, key_filter), 1.0)
        v = conv_silu(value_pad, value_filter)
        beta = jax.nn.sigmoid(beta_raw)
        log_decay = -jnp.exp(decay_log) * jax.nn.softplus(alpha_raw + step_bias)
        return q, k, v, beta, running_sum(log_decay)

    (q, k, v, beta, gc), front_back = jax.vjp(
        front, *padded, rounded[3].astype(F32), rounded[4].astype(F32)
    )
    dq, dk, dv, dbeta, dgc, dgr = recurrence_grads(q, k, v, beta, gc, gc.T, grad_core)
    grads = front_back((dq, dk, dv, dbeta, dgc + dgr.T))
    arriving = from_behind(jnp.concatenate([g[:lag] for g in grads[:3]], 1), "ctx", -1)
    full = []
    for n in range(3):
        tail = arriving[:, cuts[n] : cuts[n + 1]]
        full.append((grads[n][lag:] + jnp.pad(tail, ((rows_here - lag, 0), (0, 0)))).astype(BF))
    full += [g.astype(BF) for g in grads[3:]]

    def contribution(pieces):
        total = 0.0
        for grad_rows, weight in zip(full, pieces):
            total = total + lax.dot_general(
                grad_rows, weight, (((1,), (1,)), ((), ())), preferred_element_type=F32
            )
        return total

    share = inputs.shape[1]
    if pair:
        far = contribution(
            [lax.dynamic_slice_in_dim(w, (1 - side) * share, share, 0) for w in weights]
        ).astype(BF)
        arrived = lax.ppermute(far, "tp", [(0, 1), (1, 0)])
        near = contribution(
            [lax.dynamic_slice_in_dim(w, side * share, share, 0) for w in weights]
        )
        return (near + arrived.astype(F32)).astype(BF)
    return lax.psum_scatter(
        contribution(weights).astype(BF), "tp", scatter_dimension=1, tiled=True
    )


def solution(mesh):
    return jax.shard_map(
        local,
        mesh=mesh,
        in_specs=(
            P("ctx", "tp"),
            P(None, "tp"),
            P(None, "tp"),
            P(None, "tp"),
            P(None, "tp"),
            P(None, "tp"),
            P(None, "tp"),
            P(None, "tp"),
            P(None, "tp"),
            P("tp"),
            P("tp"),
            P("ctx", "tp"),
        ),
        out_specs=P("ctx", "tp"),
        check_vma=False,
    )
```

time: 751 us -> 125 us (0.17); the launches traced: 737 us -> 124 us
  waiting for transfers between devices: 355 us -> 5.4 us
  matrix products: 212 us -> 13.6 us
  local copies, waits for them, and re-layouts: 95.6 us -> 13.4 us
  Pallas kernels: 0 us -> 67.2 us
  other arithmetic: 38.8 us -> 17.1 us
  between operations: 15.1 us -> 0.83 us
  starting transfers between devices: 16.6 us -> 6.37 us
    all_gather x4 -> x0, waiting for transfers between devices: 331 us -> none  [entering(): pieces = jax.tree.map(lambda part: lax.all_gather(part, axis), value)]
    dot_general x111 -> x17, matrix products: 212 us -> 13.6 us  [the longest x10 8.59 us: contribution(): lax.dot_general(grad_rows, weight, (((1,), (1,)), ((), ())), preferred_el...]
    pallas_call x0 -> x1, Pallas kernels: none -> 67.2 us  [recurrence_grads(): pl.pallas_call(functools.partial(core_kernel, kheads, ratio, group), out_...]
    while x61 -> x0, local copies, waits for them, and re-layouts: 47.6 us -> none
    psum x1 -> x0, waiting for transfers between devices: 20.3 us -> none  [local(): lax.psum(partial_value.astype(jnp.bfloat16), 'tp').astype(jnp.float32)]
    rev x2 -> x0, local copies, waits for them, and re-layouts: 15.7 us -> none  [entering(): pieces = jax.tree.map(lambda part: part[::-1], pieces)]
    ppermute x6 -> x2, starting transfers between devices: 16.3 us -> 5.84 us  [from_behind(): lax.ppermute(value, axis, [(source, source + steps) for source in range(l...]
  transfers between devices with their start and end apart: 11 -> 4, of which waited for: 6 -> 3; matrix products, arithmetic and copies ran while one was open for 42% -> 4% of each run, Pallas kernels for 0% -> 0%
where the time goes in v1:
time: 125 us; the launch traced here: 124 us
  Pallas kernels  67.2 us (54%)
  other arithmetic  17.1 us (14%)
  matrix products  13.6 us (11%)
  local copies, waits for them, and re-layouts  13.4 us (11%)
  starting transfers between devices  6.37 us (5%)
  waiting for transfers between devices  5.4 us (4%)
    pallas_call x1, Pallas kernels, recurrence_grads(): pl.pallas_call(functools.partial(core_kernel, kheads, ratio, group), out_...  67.2 us
    dot_general x10, matrix products, contribution(): lax.dot_general(grad_rows, weight, (((1,), (1,)), ((), ())), preferred_el...  8.59 us
    unnamed x108, local copies, waits for them, and re-layouts  6.27 us
    mul x9, other arithmetic, conv_silu(): running = running + weight[tap].astype(F32) * padded[tap:tap + length]  6.17 us
    ppermute x2, starting transfers between devices, from_behind(): lax.ppermute(value, axis, [(source, source + steps) for source in range(l...  5.84 us
    ppermute x2, waiting for transfers between devices, from_behind(): lax.ppermute(value, axis, [(source, source + steps) for source in range(l...  5.2 us
    dot_general x5, matrix products, local(): jnp.dot(whole, w, preferred_element_type=F32).astype(BF)  4.6 us
    mul x4, local copies, waits for them, and re-layouts, normalized(): shaped * (lax.rsqrt(jnp.sum(shaped * shaped, axis=-1, keepdims=True) + EP...  3.9 us
  transfers between devices with their start and end apart: 4, of which 3 were waited for; matrix products, arithmetic and copies ran while one was open for 4% of the time, Pallas kernels for 0%

profile of v1, /device:TPU:0, one launch (start us, length us, event | category | flops | bytes accessed | tf_op | source)
XLA Modules:
  0.0 123.9 jit_solution(400044784874403281)
XLA Ops:
  0.0 0.5 collective-permute-start
  0.5 0.9 slice_convert_fusion.7
  1.4 0.8 slice_convert_fusion.10
  2.3 0.7 exponential_negate_fusion
  3.0 0.9 slice_convert_fusion.3
  3.9 3.1 %convolution_convert_fusion = bf16[128,1024]{1,0:T(8,128)(2,1)S(1)} fusion(bf16[2048,1024]{1,0:T(8,128)(2,1)} %param.15, bf16[128,1024]{1,0:T(8,128)(2,1)S(1)} %collective-permute-done, bf16[128,1024]{1,0:T(8,128)(2,1)} %param.12, pred[]{:T(512)S(6)} %eq.11), kind=kOutput, calls=%fused_computation.15 | convolution fusion | flops 539361280 | bytes 4980737 | tf_op jit(solution)/shard_map/dot_general | solution.py:339
  7.1 0.5 convolution_convert_fusion.1
  7.5 1.2 copy-done.17
  8.7 0.5 convolution_convert_fusion.2
  9.2 0.3 copy-done.23
  9.5 0.3 convolution_convert_fusion.3
  9.8 0.5 copy-done.25
  10.2 0.2 convolution_convert_fusion.4
  10.6 4.4 %collective-permute-start.1 = (bf16[3,2048]{1,0:T(4,128)(2,1)S(1)}, bf16[3,2048]{1,0:T(4,128)(2,1)S(1)}, u32[]{:S(2)}, u32[]{:S(2)}) collective-permute-start(bf16[3,2048]{1,0:T(4,128)(2,1)S(1)} %pad_maximum_fusion.1), channel_id=1, source_target_pairs={{0,2},{2,4},{4,6},{6,8},{8,10},{10,12},{12,14},{14,16},{16,18},{18... | collective-permute-start | bytes 36872 | tf_op jit(solution)/shard_map/ppermute | solution.py:292
  15.0 0.2 fusion.45
  15.2 0.1 copy.28.gc_ref
  15.4 1.0 collective-permute-done.1
  16.5 0.2 fusion.92
  16.8 0.2 reduce_sum.36
  17.1 0.1 copy.27
  17.2 1.0 maximum_convert_fusion
  18.3 1.0 fusion.90
  19.3 1.8 %mul.447 = f32[128,4,128]{2,1,0:T(4,128)} reshape(f32[128,512]{1,0:T(8,128)} %get-tuple-element.37) | data formatting | bytes 524288 | tf_op jit(solution)/shard_map/jvp()/mul | solution.py:306
  21.1 1.2 reduce_sum.35
  22.3 0.1 copy.25
  22.4 0.2 mul.471
  22.7 0.7 copy-done.6
  23.5 0.2 mul.449
  23.8 0.6 copy-done.8
  24.4 1.1 fusion.28
  25.5 67.2 %shard_map.118 = (f32[128,512]{1,0:T(8,128)S(1)}, f32[128,512]{1,0:T(8,128)S(1)}, f32[128,1024]{1,0:T(8,128)S(1)}, f32[128,8]{1,0:T(8,128)S(1)}, f32[128,8]{1,0:T(8,128)S(1)}, /*index=5*/f32[8,128]{1,0:T(8,128)S(1)}) custom-call(f32[128,512]{1,0:T(8,128)S(1)} %bitcast_multiply_fusion.5.q_ref, f32[128,512]{1,0:T(8,128)S(1)} %bitcast_multiply_fusion.3.k_ref, ...), custom_call_target="tpu_custom_call" | custom-call | tf_op jit(solution)/shard_map/pallas_call | solution.py:265
  92.8 1.0 fusion.55
  93.9 0.1 fusion.14
  94.0 1.1 fusion.53
  95.1 1.0 fusion.59
  96.2 1.1 fusion.57
  97.2 1.7 %fusion.89 = f32[128,512]{1,0:T(8,128)} fusion(f32[128,512]{1,0:T(8,128)S(1)} %get-tuple-element.21, f32[128,512]{1,0:T(8,128)} %get-tuple-element.38), kind=kLoop, calls=%fused_computation.173 | loop fusion | flops 327680 | bytes 786432 | tf_op jit(solution)/shard_map/transpose(jvp())/mul | solution.py:306
  99.0 1.8 %mul.495 = f32[128,4,128]{2,1,0:T(4,128)} reshape(f32[128,512]{1,0:T(8,128)} %fusion.89) | data formatting | bytes 524288 | tf_op jit(solution)/shard_map/transpose(jvp())/mul | solution.py:306
  100.7 1.2 reduce_sum.37
  102.1 0.2 broadcast_in_dim.16
  102.4 1.9 %broadcast_multiply_fusion.11 = (f32[128,512]{1,0:T(8,128)}, f32[128,512]{1,0:T(8,128)S(1)}) fusion(f32[512]{0:T(512)S(1)} %bitcast.91, f32[128,512]{1,0:T(8,128)} %get-tuple-element.38, f32[16,8,4,128]{3,2,1,0:T(4,128)S(1)} %bitcast.66, f32[128,512]{1,0:T(8,128)S(1)} %get-tuple-element.21, f32[16,8,4,128]{3,2,1,0:T(4,128)} %bitcast.65), kind=kLoop, calls=%fused_computation.101 | loop fusion | flops 983040 | bytes 1574912 | tf_op jit(solution)/shard_map/transpose(jvp())/mul | solution.py:300
  104.3 0.9 broadcast_multiply_fusion.8
  105.2 0.8 fusion.91
  106.0 1.7 %mul.510 = f32[128,4,128]{2,1,0:T(4,128)} reshape(f32[128,512]{1,0:T(8,128)} %fusion.91) | data formatting | bytes 524288 | tf_op jit(solution)/shard_map/transpose(jvp())/mul | solution.py:306
  107.7 1.2 reduce_sum.41
  109.1 0.2 broadcast_in_dim.20
  109.3 0.2 broadcast_multiply_fusion.4
  109.6 0.5 copy-done.19
  110.2 0.3 broadcast_multiply_fusion
  110.4 0.2 broadcast_multiply_fusion.1
  110.6 0.5 copy-done.9
  111.4 1.5 %collective-permute-start.2 = (f32[3,2048]{1,0:T(4,128)S(1)}, f32[3,2048]{1,0:T(4,128)S(1)}, u32[]{:S(2)}, u32[]{:S(2)}) collective-permute-start(f32[3,2048]{1,0:T(4,128)S(1)} %pad_maximum_fusion), channel_id=1, source_target_pairs={{2,0},{4,2},{6,4},{8,6},{10,8},{12,10},{14,12},{16,14},{18,16},{20... | collective-permute-start | bytes 73736 | tf_op jit(solution)/shard_map/ppermute | solution.py:292
  113.0 4.2 %collective-permute-done.2 = f32[3,2048]{1,0:T(4,128)S(1)} collective-permute-done((f32[3,2048]{1,0:T(4,128)S(1)}, f32[3,2048]{1,0:T(4,128)S(1)}, u32[]{:S(2)}, u32[]{:S(2)}) %collective-permute-start.2) | collective-permute-done | bytes 24608 | tf_op jit(solution)/shard_map/ppermute | solution.py:292
  117.2 0.1 fusion.34
  117.3 0.5 fusion.15
  117.9 0.2 fusion.24
  118.1 1.3 %copy-done.2 = bf16[2048,1024]{1,0:T(8,128)(2,1)S(1)} copy-done((bf16[2048,1024]{1,0:T(8,128)(2,1)S(1)}, bf16[2048,1024]{1,0:T(8,128)(2,1)}, u32[]{:S(2)}) %copy-start.2) | copy-done | bytes 4194328
  119.4 0.8 fusion
  120.2 0.3 copy-done.18
  120.5 0.5 fusion.12
  121.1 0.5 fusion.18
  121.6 0.8 fusion.2
  122.5 0.2 collective-permute-done.3
  122.7 1.2 fusion.11
  (131 shorter events, 1.7 us)
Async XLA Ops:
  0.0 7.0 %copy-start = (bf16[2048,512]{1,0:T(8,128)(2,1)S(1)}, bf16[2048,512]{1,0:T(8,128)(2,1)}, u32[]{:S(2)}) copy-start(bf16[2048,512]{1,0:T(8,128)(2,1)} %param.14) | copy-start | bytes 6291460
  0.0 3.9 %collective-permute-start = (bf16[128,1024]{1,0:T(8,128)(2,1)}, bf16[128,1024]{1,0:T(8,128)(2,1)S(1)}, u32[]{:S(2)}, u32[]{:S(2)}) collective-permute-start(bf16[128,1024]{1,0:T(8,128)(2,1)} %param.12), channel_id=1, source_target_pairs={{0,1},{1,0},{2,3},{3,2},{4,5},{5,4},{6,7},{7,6},{8,9},{9,8},{10,11... | collective-permute-start | bytes 786440 | tf_op jit(solution)/shard_map/ppermute | solution.py:330
  1.4 15.1 %copy-start.27 = (f32[1,512]{1,0:T(1,128)}, f32[1,512]{1,0:T(1,128)S(1)}, u32[]{:S(2)}) copy-start(f32[1,512]{1,0:T(1,128)S(1)} %get-tuple-element.56) | copy-start | bytes 6148
  1.4 15.1 %copy-start.29 = (f32[1,512]{1,0:T(1,128)}, f32[1,512]{1,0:T(1,128)S(1)}, u32[]{:S(2)}) copy-start(f32[1,512]{1,0:T(1,128)S(1)} %get-tuple-element.57) | copy-start | bytes 6148
  1.4 15.1 %copy-start.31 = (f32[1,512]{1,0:T(1,128)}, f32[1,512]{1,0:T(1,128)S(1)}, u32[]{:S(2)}) copy-start(f32[1,512]{1,0:T(1,128)S(1)} %get-tuple-element.59) | copy-start | bytes 6148
  1.4 15.1 %copy-start.33 = (f32[1,512]{1,0:T(1,128)}, f32[1,512]{1,0:T(1,128)S(1)}, u32[]{:S(2)}) copy-start(f32[1,512]{1,0:T(1,128)S(1)} %get-tuple-element.58) | copy-start | bytes 6148
  2.3 16.0 %copy-start.35 = (f32[1,512]{1,0:T(1,128)}, f32[1,512]{1,0:T(1,128)S(1)}, u32[]{:S(2)}) copy-start(f32[1,512]{1,0:T(1,128)S(1)} %get-tuple-element.60) | copy-start | bytes 6148
  2.3 16.0 %copy-start.37 = (f32[1,512]{1,0:T(1,128)}, f32[1,512]{1,0:T(1,128)S(1)}, u32[]{:S(2)}) copy-start(f32[1,512]{1,0:T(1,128)S(1)} %get-tuple-element.62) | copy-start | bytes 6148
  2.3 16.0 %copy-start.39 = (f32[1,512]{1,0:T(1,128)}, f32[1,512]{1,0:T(1,128)S(1)}, u32[]{:S(2)}) copy-start(f32[1,512]{1,0:T(1,128)S(1)} %get-tuple-element.63) | copy-start | bytes 6148
  2.3 16.0 %copy-start.41 = (f32[1,512]{1,0:T(1,128)}, f32[1,512]{1,0:T(1,128)S(1)}, u32[]{:S(2)}) copy-start(f32[1,512]{1,0:T(1,128)S(1)} %get-tuple-element.61) | copy-start | bytes 6148
  3.0 12.0 %copy-start.50 = (f32[8]{0:T(128)}, f32[8]{0:T(128)S(1)}, u32[]{:S(2)}) copy-start(f32[8]{0:T(128)S(1)} %exponential_negate_fusion) | copy-start | bytes 100
  3.8 20.6 %copy-start.21 = (f32[1,1024]{1,0:T(1,128)}, f32[1,1024]{1,0:T(1,128)S(1)}, u32[]{:S(2)}) copy-start(f32[1,1024]{1,0:T(1,128)S(1)} %get-tuple-element.54) | copy-start | bytes 12292
  3.8 3.2 %copy-start.47 = (bf16[128,1024]{1,0:T(8,128)(2,1)S(1)}, bf16[128,1024]{1,0:T(8,128)(2,1)}, u32[]{:S(2)}) copy-start(bf16[128,1024]{1,0:T(8,128)(2,1)} %param.12) | copy-start | bytes 786436
  7.0 3.5 %copy-start.20 = (bf16[128,1024]{1,0:T(8,128)(2,1)}, bf16[128,1024]{1,0:T(8,128)(2,1)S(1)}, u32[]{:S(2)}) copy-start(bf16[128,1024]{1,0:T(8,128)(2,1)S(1)} %convolution_convert_fusion) | copy-start | bytes 786436
  7.0 1.7 %copy-start.17 = (bf16[2048,512]{1,0:T(8,128)(2,1)S(1)}, bf16[2048,512]{1,0:T(8,128)(2,1)}, u32[]{:S(2)}) copy-start(bf16[2048,512]{1,0:T(8,128)(2,1)} %param.13) | copy-start | bytes 6291460
  8.7 0.8 copy-start.23
  9.5 0.8 copy-start.25
  9.5 5.5 %copy-start.48 = (f32[8]{0:T(128)S(1)}, f32[8]{0:T(128)}, u32[]{:S(2)}) copy-start(f32[8]{0:T(128)} %param.22) | copy-start | bytes 100
  10.5 6.0 %copy-start.52 = (bf16[128,8]{0,1:T(8,128)(2,1)}, bf16[128,8]{0,1:T(8,128)(2,1)S(1)}, u32[]{:S(2)}) copy-start(bf16[128,8]{0,1:T(8,128)(2,1)S(1)} %convolution_convert_fusion.4) | copy-start | bytes 6148
  10.6 5.8 %collective-permute-start.1 = (bf16[3,2048]{1,0:T(4,128)(2,1)S(1)}, bf16[3,2048]{1,0:T(4,128)(2,1)S(1)}, u32[]{:S(2)}, u32[]{:S(2)}) collective-permute-start(bf16[3,2048]{1,0:T(4,128)(2,1)S(1)} %pad_maximum_fusion.1), channel_id=1, source_target_pairs={{0,2},{2,4},{4,6},{6,8},{8,10},{10,12},{12,14},{14,16},{16,18},{18... | collective-permute-start | bytes 36872 | tf_op jit(solution)/shard_map/ppermute | solution.py:292
  16.7 6.0 %copy-start.3 = (f32[128,512]{1,0:T(8,128)}, f32[128,512]{1,0:T(8,128)S(1)}, u32[]{:S(2)}) copy-start(f32[128,512]{1,0:T(8,128)S(1)} %get-tuple-element.36) | copy-start | bytes 786436
  17.1 6.4 %copy-start.43 = (f32[128,4]{0,1:T(4,128)}, f32[128,4]{0,1:T(4,128)S(1)}, u32[]{:S(2)}) copy-start(f32[128,4]{0,1:T(4,128)S(1)} %copy.26) | copy-start | bytes 6148
  19.3 4.4 %copy-start.5 = (f32[128,512]{1,0:T(8,128)S(1)}, f32[128,512]{1,0:T(8,128)}, u32[]{:S(2)}) copy-start(f32[128,512]{1,0:T(8,128)} %get-tuple-element.38) | copy-start | bytes 786436
  22.3 3.2 %copy-start.45 = (f32[128,4]{0,1:T(4,128)}, f32[128,4]{0,1:T(4,128)S(1)}, u32[]{:S(2)}) copy-start(f32[128,4]{0,1:T(4,128)S(1)} %copy.24) | copy-start | bytes 6148
  22.6 0.7 copy-start.6
  23.5 2.1 %copy-start.1 = (bf16[128,1024]{1,0:T(8,128)(2,1)S(1)}, bf16[128,1024]{1,0:T(8,128)(2,1)}, u32[]{:S(2)}) copy-start(bf16[128,1024]{1,0:T(8,128)(2,1)} %do_ref.1) | copy-start | bytes 786436
  23.7 0.7 copy-start.8
  24.4 68.4 %copy-start.24 = (bf16[2048,8]{0,1:T(8,128)(2,1)S(1)}, bf16[2048,8]{0,1:T(8,128)(2,1)}, u32[]{:S(2)}) copy-start(bf16[2048,8]{0,1:T(8,128)(2,1)} %param.16) | copy-start | bytes 98308
  24.4 69.5 %copy-start.49 = (f32[8]{0:T(128)S(1)}, f32[8]{0:T(128)}, u32[]{:S(2)}) copy-start(f32[8]{0:T(128)} %param.22) | copy-start | bytes 100
  24.4 69.5 %copy-start.51 = (f32[8]{0:T(128)S(1)}, f32[8]{0:T(128)}, u32[]{:S(2)}) copy-start(f32[8]{0:T(128)} %copy-done.50) | copy-start | bytes 100
  24.4 69.4 %copy-start.53 = (bf16[128,8]{0,1:T(8,128)(2,1)S(1)}, bf16[128,8]{0,1:T(8,128)(2,1)}, u32[]{:S(2)}) copy-start(bf16[128,8]{0,1:T(8,128)(2,1)} %copy-done.52) | copy-start | bytes 6148
  24.4 69.6 %copy-start.26 = (bf16[2048,8]{0,1:T(8,128)(2,1)S(1)}, bf16[2048,8]{0,1:T(8,128)(2,1)}, u32[]{:S(2)}) copy-start(bf16[2048,8]{0,1:T(8,128)(2,1)} %param.17) | copy-start | bytes 98308
  92.8 9.2 %copy-start.46 = (f32[128,4]{0,1:T(4,128)S(1)}, f32[128,4]{0,1:T(4,128)}, u32[]{:S(2)}) copy-start(f32[128,4]{0,1:T(4,128)} %copy-done.45) | copy-start | bytes 6148
  93.9 8.5 %copy-start.42 = (f32[1,512]{1,0:T(1,128)S(1)}, f32[1,512]{1,0:T(1,128)}, u32[]{:S(2)}) copy-start(f32[1,512]{1,0:T(1,128)} %copy-done.41) | copy-start | bytes 6148
  96.1 8.1 %copy-start.36 = (f32[1,512]{1,0:T(1,128)S(1)}, f32[1,512]{1,0:T(1,128)}, u32[]{:S(2)}) copy-start(f32[1,512]{1,0:T(1,128)} %copy-done.35) | copy-start | bytes 6148
  96.1 8.1 %copy-start.38 = (f32[1,512]{1,0:T(1,128)S(1)}, f32[1,512]{1,0:T(1,128)}, u32[]{:S(2)}) copy-start(f32[1,512]{1,0:T(1,128)} %copy-done.37) | copy-start | bytes 6148
  96.1 8.1 %copy-start.40 = (f32[1,512]{1,0:T(1,128)S(1)}, f32[1,512]{1,0:T(1,128)}, u32[]{:S(2)}) copy-start(f32[1,512]{1,0:T(1,128)} %copy-done.39) | copy-start | bytes 6148
  99.0 6.2 %copy-start.4 = (f32[128,512]{1,0:T(8,128)S(1)}, f32[128,512]{1,0:T(8,128)}, u32[]{:S(2)}) copy-start(f32[128,512]{1,0:T(8,128)} %copy-done.3) | copy-start | bytes 786436
  102.3 6.6 %copy-start.44 = (f32[128,4]{0,1:T(4,128)S(1)}, f32[128,4]{0,1:T(4,128)}, u32[]{:S(2)}) copy-start(f32[128,4]{0,1:T(4,128)} %copy-done.43) | copy-start | bytes 6148
  102.3 7.0 %copy-start.34 = (f32[1,512]{1,0:T(1,128)S(1)}, f32[1,512]{1,0:T(1,128)}, u32[]{:S(2)}) copy-start(f32[1,512]{1,0:T(1,128)} %copy-done.33) | copy-start | bytes 6148
  104.2 5.1 %copy-start.7 = (f32[128,4,128]{2,1,0:T(4,128)S(1)}, f32[128,4,128]{2,1,0:T(4,128)}, u32[]{:S(2)}) copy-start(f32[128,4,128]{2,1,0:T(4,128)} %copy-done.6) | copy-start | bytes 786436
  105.2 4.3 %copy-start.28 = (f32[1,512]{1,0:T(1,128)S(1)}, f32[1,512]{1,0:T(1,128)}, u32[]{:S(2)}) copy-start(f32[1,512]{1,0:T(1,128)} %copy-done.27) | copy-start | bytes 6148
  105.2 4.3 %copy-start.30 = (f32[1,512]{1,0:T(1,128)S(1)}, f32[1,512]{1,0:T(1,128)}, u32[]{:S(2)}) copy-start(f32[1,512]{1,0:T(1,128)} %copy-done.29) | copy-start | bytes 6148
  105.2 4.3 %copy-start.32 = (f32[1,512]{1,0:T(1,128)S(1)}, f32[1,512]{1,0:T(1,128)}, u32[]{:S(2)}) copy-start(f32[1,512]{1,0:T(1,128)} %copy-done.31) | copy-start | bytes 6148
  106.0 3.7 %copy-start.22 = (f32[1,1024]{1,0:T(1,128)S(1)}, f32[1,1024]{1,0:T(1,128)}, u32[]{:S(2)}) copy-start(f32[1,1024]{1,0:T(1,128)} %copy-done.21) | copy-start | bytes 12292
  109.1 1.0 copy-start.19
  110.1 0.9 copy-start.9
  110.1 1.0 copy-start.10
  110.2 1.1 copy-start.11
  110.2 1.2 copy-start.12
  111.4 5.8 %collective-permute-start.2 = (f32[3,2048]{1,0:T(4,128)S(1)}, f32[3,2048]{1,0:T(4,128)S(1)}, u32[]{:S(2)}, u32[]{:S(2)}) collective-permute-start(f32[3,2048]{1,0:T(4,128)S(1)} %pad_maximum_fusion), channel_id=1, source_target_pairs={{2,0},{4,2},{6,4},{8,6},{10,8},{12,10},{14,12},{16,14},{18,16},{20... | collective-permute-start | bytes 73736 | tf_op jit(solution)/shard_map/ppermute | solution.py:292
  117.2 2.2 %copy-start.2 = (bf16[2048,1024]{1,0:T(8,128)(2,1)S(1)}, bf16[2048,1024]{1,0:T(8,128)(2,1)}, u32[]{:S(2)}) copy-start(bf16[2048,1024]{1,0:T(8,128)(2,1)} %param.15) | copy-start | bytes 12582916
  117.8 2.4 %copy-start.15 = (f32[128,1024]{1,0:T(8,128)S(1)}, f32[128,1024]{1,0:T(8,128)}, u32[]{:S(2)}) copy-start(f32[128,1024]{1,0:T(8,128)} %fusion.55) | copy-start | bytes 1572868
  117.8 2.4 %copy-start.16 = (f32[128,1024]{1,0:T(8,128)S(1)}, f32[128,1024]{1,0:T(8,128)}, u32[]{:S(2)}) copy-start(f32[128,1024]{1,0:T(8,128)} %fusion.53) | copy-start | bytes 1572868
  117.8 2.7 %copy-start.18 = (bf16[2048,512]{1,0:T(8,128)(2,1)S(1)}, bf16[2048,512]{1,0:T(8,128)(2,1)}, u32[]{:S(2)}) copy-start(bf16[2048,512]{1,0:T(8,128)(2,1)} %param.13) | copy-start | bytes 6291460
  121.1 1.6 %copy-start.13 = (f32[128,1024]{1,0:T(8,128)S(1)}, f32[128,1024]{1,0:T(8,128)}, u32[]{:S(2)}) copy-start(f32[128,1024]{1,0:T(8,128)} %fusion.59) | copy-start | bytes 1572868
  121.1 1.6 %copy-start.14 = (f32[128,1024]{1,0:T(8,128)S(1)}, f32[128,1024]{1,0:T(8,128)}, u32[]{:S(2)}) copy-start(f32[128,1024]{1,0:T(8,128)} %fusion.57) | copy-start | bytes 1572868
  121.1 1.6 %collective-permute-start.3 = (bf16[128,1024]{1,0:T(8,128)(2,1)S(1)}, bf16[128,1024]{1,0:T(8,128)(2,1)S(1)}, u32[]{:S(2)}, u32[]{:S(2)}) collective-permute-start(bf16[128,1024]{1,0:T(8,128)(2,1)S(1)} %fusion.12), channel_id=1, source_target_pairs={{0,1},{1,0},{2,3},{3,2},{4,5},{5,4},{6,7},{7,6},{8,9},{9,8},{10,11... | collective-permute-start | bytes 786440 | tf_op jit(solution)/shard_map/ppermute | solution.py:382

commit v2 on v1

--- a/solution.py
+++ b/solution.py
@@ -68,14 +68,18 @@
 
 def core_kernel(
     kheads, ratio, group,
-    q_ref, k_ref, v_ref, beta_ref, gc_ref, gr_ref, do_ref,
-    dq_ref, dk_ref, dv_ref, dbeta_ref, dgc_ref, dgr_ref,
-    inv_s, w_s, vm_s, y_s, move_s, add_s, end_s, land_s, out_s,
+    pq_ref, pk_ref, pv_ref, taps_ref, beta_ref, gc_ref, gr_ref, do_ref,
+    dpq_ref, dpk_ref, dpv_ref, dbeta_ref, dgc_ref, dgr_ref,
+    q_ref, k_ref, v_ref, pad_s, run_s, dpad_s, tail_s, tail_land, dtail_land,
+    tail_sems, inv_s, w_s, vm_s, y_s, move_s, add_s, end_s, land_s, out_s,
     send_sem, recv_sem,
 ):
     count, me = lax.axis_size("ctx"), lax.axis_index("ctx")
     vheads = kheads * ratio
-    size = q_ref.shape[0]
+    size = pq_ref.shape[0]
+    kw, vw = pq_ref.shape[1], pv_ref.shape[1]
+    width = 2 * kw + vw
+    projected = ((pq_ref, 0, kw), (pk_ref, kw, kw), (pv_ref, 2 * kw, vw))
     row = lax.broadcasted_iota(jnp.int32, (size, size), 0)
     col = lax.broadcasted_iota(jnp.int32, (size, size), 1)
     lower, strictly = row >= col, row > col
@@ -89,6 +93,83 @@
     @pl.when(me < count - 1)
     def _():
         pl.semaphore_signal(barrier, inc=1, device_id={"ctx": me + 1}, device_id_type=MESH)
+
+    peers = jnp.minimum(me, 1) + jnp.minimum(count - 1 - me, 1)
+    pl.semaphore_wait(barrier, peers)
+
+    def tail_copy():
+        return pltpu.make_async_remote_copy(
+            src_ref=tail_s, dst_ref=tail_land, send_sem=tail_sems.at[0], recv_sem=tail_sems.at[1],
+            device_id={"ctx": me + 1}, device_id_type=MESH,
+        )
+
+    def dtail_copy():
+        return pltpu.make_async_remote_copy(
+            src_ref=dpad_s.at[0:8], dst_ref=dtail_land, send_sem=tail_sems.at[2],
+            recv_sem=tail_sems.at[3], device_id={"ctx": me - 1}, device_id_type=MESH,
+        )
+
+    for ref, at, wide in projected:
+        tail_s[:, at : at + wide] = ref[size - 16 : size, :]
+
+    @pl.when(me < count - 1)
+    def _():
+        tail_copy().start()
+
+    for ref, at, wide in projected:
+        pad_s[16 : 16 + size, at : at + wide] = ref[...].astype(F32)
+    run_s[0:8, :] = jnp.zeros((8, width), F32)
+    run_s[8 + size : 16 + size, :] = jnp.zeros((8, width), F32)
+
+    @pl.when(me == 0)
+    def _():
+        tail_land[...] = jnp.zeros(tail_land.shape, tail_land.dtype)
+
+    @pl.when(me == count - 1)
+    def _():
+        dtail_land[...] = jnp.zeros(dtail_land.shape, dtail_land.dtype)
+
+    @pl.when(me > 0)
+    def _():
+        tail_copy().wait_recv()
+
+    pad_s[0:16, :] = tail_land[...].astype(F32)
+
+    def convolved(block):
+        lanes = lane_block(block)
+        taps = taps_ref[:, lanes]
+        total = taps[0:1, :] * pad_s[16 - CONV + 1 : 16 - CONV + 1 + size, lanes]
+        for tap in range(1, CONV):
+            first = 16 - CONV + 1 + tap
+            total += taps[tap : tap + 1, :] * pad_s[first : first + size, lanes]
+        gate = 1.0 / (1.0 + jnp.exp(-total))
+        return total, gate
+
+    def unit(act):
+        return lax.rsqrt(rowsum(act * act) + EPS)
+
+    def front_qk(head, carry):
+        for ref, first, scale in ((q_ref, 0, DH ** (-0.5)), (k_ref, kheads, 1.0)):
+            total, gate = convolved(first + head)
+            act = total * gate
+            ref[:, lane_block(head)] = act * (unit(act) * scale)
+        return carry
+
+    def front_v(head, carry):
+        total, gate = convolved(2 * kheads + head)
+        v_ref[:, lane_block(head)] = total * gate
+        return carry
+
+    lax.fori_loop(0, kheads, front_qk, 0)
+    lax.fori_loop(0, vheads, front_v, 0)
+
+    def front_back(block, grad, scale):
+        total, gate = convolved(block)
+        if scale is not None:
+            act = total * gate
+            length = unit(act)
+            grad = (scale * length) * (grad - act * (length * length * rowsum(act * grad)))
+        run_s[8 : 8 + size, lane_block(block)] = grad * (gate * (1.0 + total * (1.0 - gate)))
 
     def gates(head):
         gc, gr = column(gc_ref, head), gr_ref[pl.ds(head, 1), :]
@@ -126,9 +207,6 @@
         return carry
 
     lax.fori_loop(0, kheads // group, prepare, 0)
-
-    peers = jnp.minimum(me, 1) + jnp.minimum(count - 1 - me, 1)
-    pl.semaphore_wait(barrier, peers)
 
     @pl.when(me == 0)
     def _():
@@ -227,18 +305,61 @@
             dgc += jnp.where(at_end, colsum(dtail) + dend, 0.0)
             dq[i] += gam * dqs[n]
             dk[i] += tail * dkt[n] - dxs[n]
-            dv_ref[:, lane_block(h)] = beta * drs[n]
+            front_back(2 * kheads + h, beta * drs[n], None)
             dbeta_ref[...] += jnp.where(gate_lanes == h, dbeta, 0.0)
             dgc_ref[...] += jnp.where(gate_lanes == h, dgc, 0.0)
             dgr_ref[pl.ds(h, 1), :] = -colsum(logs)
         for i in range(group):
-            dq_ref[:, lane_block(kh[i])] = dq[i] + nn(dqk[i], ks[i])
-            dk_ref[:, lane_block(kh[i])] = (
-                dk[i] + tn(dqk[i], qs[i]) + nn(dkk[i], ks[i]) + tn(dkk[i], ks[i])
+            front_back(kh[i], dq[i] + nn(dqk[i], ks[i]), DH ** (-0.5))
+            front_back(
+                kheads + kh[i],
+                dk[i] + tn(dqk[i], qs[i]) + nn(dkk[i], ks[i]) + tn(dkk[i], ks[i]),
+                1.0,
             )
         return carry
 
     lax.fori_loop(0, kheads // group, back, 0)
+
+    def transposed(block, carry):
+        lanes = lane_block(block)
+        taps = taps_ref[:, lanes]
+        total = taps[0:1, :] * run_s[CONV - 1 : CONV + 7 + size, lanes]
+        for tap in range(1, CONV):
+            first = CONV - 1 - tap
+            total += taps[tap : tap + 1, :] * run_s[first : first + 8 + size, lanes]
+        dpad_s[:, lanes] = total
+        return carry
+
+    lax.fori_loop(0, width // DH, transposed, 0)
+
+    @pl.when(me > 0)
+    def _():
+        dtail_copy().start()
+
+    cut = size - 16
+    for ref, at, wide in ((dpq_ref, 0, kw), (dpk_ref, kw, kw), (dpv_ref, 2 * kw, vw)):
+        ref[0:cut, :] = dpad_s[8 : 8 + cut, at : at + wide].astype(BF)
+
+    @pl.when(me < count - 1)
+    def _():
+        dtail_copy().wait_recv()
+
+    for ref, at, wide in ((dpq_ref, 0, kw), (dpk_ref, kw, kw), (dpv_ref, 2 * kw, vw)):
+        ref[cut:size, :] = jnp.concatenate(
+            [
+                dpad_s[8 + cut : size, at : at + wide],
+                dpad_s[size : 8 + size, at : at + wide] + dtail_land[:, at : at + wide],
+            ],
+            0,
+        ).astype(BF)
+
+    @pl.when(me < count - 1)
+    def _():
+        tail_copy().wait_send()
+
+    @pl.when(me > 0)
+    def _():
+        dtail_copy().wait_send()
 
     def drain(head, carry):
         @pl.when(me < count - 1)
@@ -254,20 +375,31 @@
     lax.fori_loop(0, vheads, drain, 0)
 
 
-def recurrence_grads(q, k, v, beta, gc, gr, grad_core):
+def recurrence_grads(q, k, v, taps, beta, gc, gr, grad_core):
     size = q.shape[0]
+    width = taps.shape[1]
     kheads, vheads = q.shape[1] // DH, v.shape[1] // DH
     ratio = vheads // kheads
     group = 2 if kheads % 2 == 0 else 1
-    shapes = [q, k, v, beta, gc, gr]
+    shapes = [(q, BF), (k, BF), (v, BF), (beta, F32), (gc, F32), (gr, F32)]
     square = (DH, DH)
     vmem = pl.BlockSpec(memory_space=pltpu.VMEM)
     return pl.pallas_call(
         functools.partial(core_kernel, kheads, ratio, group),
-        out_shape=[jax.ShapeDtypeStruct(a.shape, F32) for a in shapes],
-        in_specs=[vmem] * 7,
+        out_shape=[jax.ShapeDtypeStruct(a.shape, kind) for a, kind in shapes],
+        in_specs=[vmem] * 8,
         out_specs=[vmem] * 6,
         scratch_shapes=[
+            pltpu.VMEM(q.shape, F32),
+            pltpu.VMEM(k.shape, F32),
+            pltpu.VMEM(v.shape, F32),
+            pltpu.VMEM((size + 16, width), F32),
+            pltpu.VMEM((size + 16, width), F32),
+            pltpu.VMEM((size + 8, width), F32),
+            pltpu.VMEM((16, width), BF),
+            pltpu.VMEM((16, width), BF),
+            pltpu.VMEM((8, width), F32),
+            pltpu.SemaphoreType.DMA((4,)),
             pltpu.VMEM((vheads, size, size), BF),
             pltpu.VMEM((vheads, size, DH), BF),
             pltpu.VMEM((vheads, size, DH), F32),
@@ -283,28 +415,7 @@
         compiler_params=pltpu.CompilerParams(
             collective_id=0, has_side_effects=True, vmem_limit_bytes=40 * 1024 * 1024
         ),
-    )(q, k, v, beta, gc, gr, grad_core)
-
-
-def from_behind(value, axis, steps):
-    count = lax.axis_size(axis)
-    leading, last = (max(0, -steps), min(count, count - steps))
-    return lax.ppermute(value, axis, [(source, source + steps) for source in range(leading, last)])
-
-
-def conv_silu(padded, weight):
-    tap_count = weight.shape[0]
-    length = padded.shape[0] - tap_count + 1
-    running = jnp.zeros((length, padded.shape[1]), F32)
-    for tap in range(tap_count):
-        running = running + weight[tap].astype(F32) * padded[tap : tap + length]
-    return jax.nn.silu(running)
-
-
-def normalized(rows_in, scale):
-    shaped = rows_in.reshape(rows_in.shape[0], -1, DH)
-    unit = shaped * (lax.rsqrt(jnp.sum(shaped * shaped, axis=-1, keepdims=True) + EPS) * scale)
-    return unit.reshape(rows_in.shape)
+    )(q, k, v, taps, beta, gc, gr, grad_core)
 
 
 def running_sum(log_decay):
@@ -321,8 +432,6 @@
     inputs, query_weight, key_weight, value_weight, beta_weight, alpha_weight,
     query_filter, key_filter, value_filter, decay_log, step_bias, grad_core,
 ):
-    rows_here = inputs.shape[0]
-    lag = CONV - 1
     weights = (query_weight, key_weight, value_weight, beta_weight, alpha_weight)
     pair = lax.axis_size("tp") == 2
     side = lax.axis_index("tp")
@@ -338,33 +447,19 @@
     rounded = lax.optimization_barrier(
         tuple(jnp.dot(whole, w, preferred_element_type=F32).astype(BF) for w in weights)
     )
-    tails = from_behind(
-        jnp.concatenate([m[rows_here - lag :] for m in rounded[:3]], 1), "ctx", 1
-    )
-    widths = [m.shape[1] for m in rounded[:3]]
-    cuts = [0, widths[0], widths[0] + widths[1], sum(widths)]
-    tails = [tails[:, cuts[n] : cuts[n + 1]] for n in range(3)]
-    padded = [jnp.concatenate([t, m], 0).astype(F32) for t, m in zip(tails, rounded)]
-
-    def front(query_pad, key_pad, value_pad, beta_raw, alpha_raw):
-        q = normalized(conv_silu(query_pad, query_filter), DH ** (-0.5))
-        k = normalized(conv_silu(key_pad, key_filter), 1.0)
-        v = conv_silu(value_pad, value_filter)
+    taps = jnp.concatenate([query_filter, key_filter, value_filter], 1).astype(F32)
+
+    def front(beta_raw, alpha_raw):
         beta = jax.nn.sigmoid(beta_raw)
         log_decay = -jnp.exp(decay_log) * jax.nn.softplus(alpha_raw + step_bias)
-        return q, k, v, beta, running_sum(log_decay)
-
-    (q, k, v, beta, gc), front_back = jax.vjp(
-        front, *padded, rounded[3].astype(F32), rounded[4].astype(F32)
+        return beta, running_sum(log_decay)
+
+    (beta, gc), front_vjp = jax.vjp(front, rounded[3].astype(F32), rounded[4].astype(F32))
+    dq, dk, dv, dbeta, dgc, dgr = recurrence_grads(
+        *rounded[:3], taps, beta, gc, gc.T, grad_core
     )
-    dq, dk, dv, dbeta, dgc, dgr = recurrence_grads(q, k, v, beta, gc, gc.T, grad_core)
-    grads = front_back((dq, dk, dv, dbeta, dgc + dgr.T))
-    arriving = from_behind(jnp.concatenate([g[:lag] for g in grads[:3]], 1), "ctx", -1)
-    full = []
-    for n in range(3):
-        tail = arriving[:, cuts[n] : cuts[n + 1]]
-        full.append((grads[n][lag:] + jnp.pad(tail, ((rows_here - lag, 0), (0, 0)))).astype(BF))
-    full += [g.astype(BF) for g in grads[3:]]
+    grads = front_vjp((dbeta, dgc + dgr.T))
+    full = [dq, dk, dv] + [g.astype(BF) for g in grads]
 
     def contribution(pieces):
         total = 0.0

time: 125 us -> 96.6 us (0.77)
  other arithmetic: 17.1 us -> 1.8 us
  local copies, waits for them, and re-layouts: 13.4 us -> 0.68 us
  Pallas kernels: 67.2 us -> 75.3 us
  starting transfers between devices: 6.37 us -> 0.52 us
  waiting for transfers between devices: 5.4 us -> 1 us
  matrix products: 13.6 us -> 16.8 us
    mul x19 -> x0, other arithmetic: 11.1 us -> none  [the longest x9 6.17 us: conv_silu(): running = running + weight[tap].astype(F32) * padded[tap:tap + length]]
    pallas_call x1, Pallas kernels: 67.2 us -> 75.3 us  [recurrence_grads(): pl.pallas_call(functools.partial(core_kernel, kheads, ratio, group), out_...]
    mul x9 -> x0, local copies, waits for them, and re-layouts: 6.15 us -> none  [the longest x4 3.9 us: normalized(): shaped * (lax.rsqrt(jnp.sum(shaped * shaped, axis=-1, keepdims=True) + EP...]
    ppermute x2 -> x0, starting transfers between devices: 5.84 us -> none  [from_behind(): lax.ppermute(value, axis, [(source, source + steps) for source in range(l...]
    unnamed x108 -> x26, local copies, waits for them, and re-layouts: 6.27 us -> 0.49 us
    ppermute x2 -> x0, waiting for transfers between devices: 5.2 us -> none  [from_behind(): lax.ppermute(value, axis, [(source, source + steps) for source in range(l...]
    reduce_sum x4 -> x0, other arithmetic: 3.68 us -> none  [the longest x2 2.32 us: normalized(): shaped * (lax.rsqrt(jnp.sum(shaped * shaped, axis=-1, keepdims=True) + EP...]
    dot_general x10, matrix products: 8.59 us -> 11.9 us  [contribution(): lax.dot_general(grad_rows, weight, (((1,), (1,)), ((), ())), preferred_el...]
  transfers between devices with their start and end apart: 4 -> 2, of which waited for: 3 -> 1; matrix products, arithmetic and copies ran while one was open for 4% -> 2% of each run, Pallas kernels for 0% -> 0%
where the time goes in v2:
time: 96.6 us; the launch traced here: 96.4 us
  Pallas kernels  75.3 us (78%)
  matrix products  16.8 us (17%)
  other arithmetic  1.8 us (2%)
  waiting for transfers between devices  1 us (1%)
    pallas_call x1, Pallas kernels, recurrence_grads(): pl.pallas_call(functools.partial(core_kernel, kheads, ratio, group), out_...  75.3 us
    dot_general x10, matrix products, contribution(): lax.dot_general(grad_rows, weight, (((1,), (1,)), ((), ())), preferred_el...  11.9 us
    dot_general x5, matrix products, local(): jnp.dot(whole, w, preferred_element_type=F32).astype(BF)  4.5 us
  transfers between devices with their start and end apart: 2, of which 1 were waited for; matrix products, arithmetic and copies ran while one was open for 2% of the time, Pallas kernels for 0%

profile of v2, /device:TPU:0, one launch (start us, length us, event | category | flops | bytes accessed | tf_op | source)
XLA Modules:
  0.0 96.4 jit_solution(7444601980978749832)
XLA Ops:
  0.0 0.0 copy-start
  0.0 0.0 copy-start.9
  0.0 0.5 collective-permute-start
  0.5 0.9 exponential_negate_fusion
  1.3 0.0 copy-start.4
  1.3 0.9 maximum_convert_fusion.taps_ref
  2.2 0.0 collective-permute-done
  2.2 0.0 copy-done
  2.2 0.0 copy-start.10
  2.3 0.0 copy-start.2
  2.3 1.6 %convolution_convert_fusion.2.pq_ref = bf16[128,512]{1,0:T(8,128)(2,1)S(1)} fusion(bf16[2048,512]{1,0:T(8,128)(2,1)S(1)} %copy-done, bf16[128,1024]{1,0:T(8,128)(2,1)S(1)} %collective-permute-done, bf16[128,1024]{1,0:T(8,128)(2,1)} %param.12, pred[]{:T(512)S(6)} %eq.11), kind=kOutput, calls=%fused_computation.15 | convolution fusion | flops 270860288 | bytes 2752513 | tf_op jit(solution)/shard_map/dot_general | solution.py:448
  3.9 0.0 copy-done.9
  3.9 0.0 copy-done.4
  3.9 0.5 convolution_convert_fusion.1.pk_ref
  4.4 0.0 copy-done.10
  4.4 0.4 copy-done.2
  4.9 0.0 copy-start.8
  4.9 0.8 convolution_convert_fusion.pv_ref
  5.6 0.0 copy-done.8
  5.6 0.0 copy-start.7
  5.7 0.0 copy-start.11
  5.7 0.0 copy-start.12
  5.7 0.0 copy-start.1
  5.7 1.4 %convolution_convert_fusion.3 = bf16[128,8]{1,0:T(8,128)(2,1)S(1)} fusion(bf16[2048,8]{0,1:T(8,128)(2,1)S(1)} %copy-done.8, bf16[128,1024]{1,0:T(8,128)(2,1)} %copy-done.10, bf16[128,1024]{1,0:T(8,128)(2,1)S(1)} %copy-done.9, pred[]{:T(512)S(6)} %eq.11), kind=kOutput, calls=%fused_computation.16 | convolution fusion | flops 6554624 | bytes 559105 | tf_op jit(solution)/shard_map/dot_general | solution.py:448
  7.1 0.0 copy-done.7
  7.1 0.0 copy-done.11
  7.1 0.2 convolution_convert_fusion.4
  7.4 0.0 copy-done.12
  7.4 0.2 fusion.18
  7.6 0.1 copy.14.gc_ref
  7.8 0.0 copy-done.1
  7.8 0.0 copy-start.3
  7.8 75.3 %shard_map.118 = (bf16[128,512]{1,0:T(8,128)(2,1)S(1)}, bf16[128,512]{1,0:T(8,128)(2,1)S(1)}, bf16[128,1024]{1,0:T(8,128)(2,1)S(1)}, f32[128,8]{1,0:T(8,128)S(1)...) custom-call(bf16[128,512]{1,0:T(8,128)(2,1)S(1)} %convolution_convert_fusion.2.pq_ref, ...), custom_call_target="tpu_custom_call" | custom-call | tf_op jit(solution)/shard_map/pallas_call | solution.py:387
  83.1 1.0 %fusion.27 = f32[128,1024]{1,0:T(8,128)} fusion(bf16[2048,8]{0,1:T(8,128)(2,1)S(1)} %copy-done.8, s32[]{:T(128)S(6)} %select_n.47, f32[128,8]{1,0:T(8,128)S(1)} %get-tuple-element.24, bf16[128,8]{1,0:T(8,128)(2,1)S(1)} %convolution_convert_fusion.3), kind=kOutput, calls=%fused_computation.43 | convolution fusion | flops 2105344 | bytes 638980 | tf_op jit(solution)/shard_map/dot_general | solution.py:467
  84.1 3.2 %fusion = f32[128,1024]{1,0:T(8,128)} fusion(bf16[128,1024]{1,0:T(8,128)(2,1)S(1)} %get-tuple-element.23, bf16[2048,1024]{1,0:T(8,128)(2,1)} %param.15, s32[]{:T(128)S(6)} %select_n.47), kind=kOutput, calls=%fused_computation | convolution fusion | flops 268435456 | bytes 2883588 | tf_op jit(solution)/shard_map/dot_general | solution.py:467
  87.4 0.2 fusion.32
  87.6 0.0 copy-done.3
  87.6 1.6 %fusion.2 = f32[128,1024]{1,0:T(8,128)} fusion(bf16[128,1024]{1,0:T(8,128)(2,1)S(1)} %get-tuple-element.23, bf16[2048,1024]{1,0:T(8,128)(2,1)S(1)} %copy-done.3, s32[]{:T(128)S(6)} %select_n.44), kind=kOutput, calls=%fused_computation.2 | convolution fusion | flops 268435456 | bytes 2883588 | tf_op jit(solution)/shard_map/dot_general | solution.py:467
  89.2 1.3 %fusion.12 = f32[128,1024]{1,0:T(8,128)} fusion(bf16[128,512]{1,0:T(8,128)(2,1)S(1)} %get-tuple-element.21, bf16[2048,512]{1,0:T(8,128)(2,1)S(1)} %copy-done, s32[]{:T(128)S(6)} %select_n.47), kind=kOutput, calls=%fused_computation.22 | convolution fusion | flops 134217728 | bytes 1703940 | tf_op jit(solution)/shard_map/dot_general | solution.py:467
  90.5 0.5 fusion.15
  91.0 0.0 copy-start.5
  91.0 0.0 copy-start.6
  91.0 0.2 fusion.10
  91.2 2.3 %fusion.7 = f32[128,1024]{1,0:T(8,128)S(1)} fusion(f32[128,1024]{1,0:T(8,128)} %fusion.27, f32[128,1024]{1,0:T(8,128)} %fusion, f32[128,1024]{1,0:T(8,128)} %fusion.12, bf16[128,512]{1,0:T(8,128)(2,1)S(1)} %get-tuple-element.22, bf16[2048,512]{1,0:T(8,128)(2,1)} %param.14, s32[]{:T(128)S(6)} %select_n.47), kind=kOutput, calls=%fused_computation.9 | convolution fusion | flops 134610944 | bytes 3276804 | tf_op jit(solution)/shard_map/dot_general | solution.py:467
  93.5 0.3 fusion.8
  93.8 0.1 collective-permute-start.1
  93.9 0.0 copy-done.5
  93.9 0.0 copy-done.6
  93.9 0.5 fusion.5
  94.4 1.0 %collective-permute-done.1 = bf16[128,1024]{1,0:T(8,128)(2,1)S(1)} collective-permute-done((bf16[128,1024]{1,0:T(8,128)(2,1)S(1)}, bf16[128,1024]{1,0:T(8,128)(2,1)S(1)}, u32[]{:S(2)}, u32[]{:S(2)}) %collective-permute-start.1) | collective-permute-done | bytes 262176 | tf_op jit(solution)/shard_map/ppermute | solution.py:477
  95.4 1.0 %add_convert_fusion = bf16[128,1024]{1,0:T(8,128)(2,1)} fusion(bf16[128,1024]{1,0:T(8,128)(2,1)S(1)} %collective-permute-done.1, f32[128,1024]{1,0:T(8,128)S(1)} %fusion.5, bf16[128,8]{0,1:T(8,128)(2,1)S(1)} %fusion.10, bf16[2048,8]{0,1:T(8,128)(2,1)S(1)} %copy-done.7, s32[]{:T(128)S(6)} %select_n.44), kind=kOutput, calls=%fused_computation.28 | convolution fusion | flops 2621440 | bytes 1067012 | tf_op jit(solution)/shard_map/dot_general | solution.py:467
  (2 shorter events, 0.1 us)
Async XLA Ops:
  0.0 2.2 %copy-start = (bf16[2048,512]{1,0:T(8,128)(2,1)S(1)}, bf16[2048,512]{1,0:T(8,128)(2,1)}, u32[]{:S(2)}) copy-start(bf16[2048,512]{1,0:T(8,128)(2,1)} %param.13) | copy-start | bytes 6291460
  0.0 3.9 %copy-start.9 = (bf16[128,1024]{1,0:T(8,128)(2,1)S(1)}, bf16[128,1024]{1,0:T(8,128)(2,1)}, u32[]{:S(2)}) copy-start(bf16[128,1024]{1,0:T(8,128)(2,1)} %param.12) | copy-start | bytes 786436
  0.0 2.2 %collective-permute-start = (bf16[128,1024]{1,0:T(8,128)(2,1)}, bf16[128,1024]{1,0:T(8,128)(2,1)S(1)}, u32[]{:S(2)}, u32[]{:S(2)}) collective-permute-start(bf16[128,1024]{1,0:T(8,128)(2,1)} %param.12), channel_id=1, source_target_pairs={{0,1},{1,0},{2,3},{3,2},{4,5},{5,4},{6,7},{7,6},{8,9},{9,8},{10,11... | collective-permute-start | bytes 786440 | tf_op jit(solution)/shard_map/ppermute | solution.py:439
  1.3 2.6 %copy-start.4 = (bf16[2048,512]{1,0:T(8,128)(2,1)S(1)}, bf16[2048,512]{1,0:T(8,128)(2,1)}, u32[]{:S(2)}) copy-start(bf16[2048,512]{1,0:T(8,128)(2,1)} %param.14) | copy-start | bytes 6291460
  2.2 2.2 %copy-start.10 = (bf16[128,1024]{1,0:T(8,128)(2,1)}, bf16[128,1024]{1,0:T(8,128)(2,1)S(1)}, u32[]{:S(2)}) copy-start(bf16[128,1024]{1,0:T(8,128)(2,1)S(1)} %collective-permute-done) | copy-start | bytes 786436
  2.3 2.6 %copy-start.2 = (bf16[2048,1024]{1,0:T(8,128)(2,1)S(1)}, bf16[2048,1024]{1,0:T(8,128)(2,1)}, u32[]{:S(2)}) copy-start(bf16[2048,1024]{1,0:T(8,128)(2,1)} %param.15) | copy-start | bytes 12582916
  4.9 0.8 copy-start.8
  5.6 1.4 %copy-start.7 = (bf16[2048,8]{0,1:T(8,128)(2,1)S(1)}, bf16[2048,8]{0,1:T(8,128)(2,1)}, u32[]{:S(2)}) copy-start(bf16[2048,8]{0,1:T(8,128)(2,1)} %param.17) | copy-start | bytes 98308
  5.7 1.4 %copy-start.11 = (bf16[128,1024]{1,0:T(8,128)(2,1)S(1)}, bf16[128,1024]{1,0:T(8,128)(2,1)}, u32[]{:S(2)}) copy-start(bf16[128,1024]{1,0:T(8,128)(2,1)} %copy-done.10) | copy-start | bytes 786436
  5.7 1.7 %copy-start.12 = (f32[8]{0:T(128)S(1)}, f32[8]{0:T(128)}, u32[]{:S(2)}) copy-start(f32[8]{0:T(128)} %param.22) | copy-start | bytes 100
  5.7 2.1 %copy-start.1 = (bf16[128,1024]{1,0:T(8,128)(2,1)S(1)}, bf16[128,1024]{1,0:T(8,128)(2,1)}, u32[]{:S(2)}) copy-start(bf16[128,1024]{1,0:T(8,128)(2,1)} %do_ref.1) | copy-start | bytes 786436
  7.8 79.8 %copy-start.3 = (bf16[2048,1024]{1,0:T(8,128)(2,1)S(1)}, bf16[2048,1024]{1,0:T(8,128)(2,1)}, u32[]{:S(2)}) copy-start(bf16[2048,1024]{1,0:T(8,128)(2,1)} %param.15) | copy-start | bytes 12582916
  91.0 2.9 %copy-start.5 = (bf16[2048,512]{1,0:T(8,128)(2,1)S(1)}, bf16[2048,512]{1,0:T(8,128)(2,1)}, u32[]{:S(2)}) copy-start(bf16[2048,512]{1,0:T(8,128)(2,1)} %param.14) | copy-start | bytes 6291460
  91.0 2.9 %copy-start.6 = (f32[128,1024]{1,0:T(8,128)S(1)}, f32[128,1024]{1,0:T(8,128)}, u32[]{:S(2)}) copy-start(f32[128,1024]{1,0:T(8,128)} %fusion.2) | copy-start | bytes 1572868
  93.8 1.6 %collective-permute-start.1 = (bf16[128,1024]{1,0:T(8,128)(2,1)S(1)}, bf16[128,1024]{1,0:T(8,128)(2,1)S(1)}, u32[]{:S(2)}, u32[]{:S(2)}) collective-permute-start(bf16[128,1024]{1,0:T(8,128)(2,1)S(1)} %fusion.8), channel_id=1, source_target_pairs={{0,1},{1,0},{2,3},{3,2},{4,5},{5,4},{6,7},{7,6},{8,9},{9,8},{10,11... | collective-permute-start | bytes 786440 | tf_op jit(solution)/shard_map/ppermute | solution.py:477

commit v3 on v2

--- a/solution.py
+++ b/solution.py
@@ -228,9 +228,7 @@
             device_id_type=MESH,
         )
 
-    def chain(step, carry):
-        turn, head = step // vheads, step % vheads
-        way = turn + late - 2 * turn * late
+    def advance(way, head):
         before, after = me - 1 + 2 * way, me + 1 - 2 * way
 
         @pl.when((before >= 0) & (before < count))
@@ -247,9 +245,24 @@
             ).astype(BF)
             hop(way, head, after).start()
 
-        return carry
-
-    lax.fori_loop(0, 2 * vheads, chain, 0)
+    lag = jnp.minimum(vheads, 2 * (1 - 2 * late) * (count - 1 - 2 * me))
+
+    def leading(head, carry):
+        advance(late, head)
+        return carry
+
+    def mixed(head, carry):
+        advance(1 - late, head)
+        advance(late, lag + head)
+        return carry
+
+    def trailing(head, carry):
+        advance(1 - late, head)
+        return carry
+
+    lax.fori_loop(0, lag, leading, 0)
+    lax.fori_loop(0, vheads - lag, mixed, 0)
+    lax.fori_loop(vheads - lag, vheads, trailing, 0)
 
     dbeta_ref[...] = jnp.zeros(dbeta_ref.shape, F32)
     dgc_ref[...] = jnp.zeros(dgc_ref.shape, F32)
@@ -461,26 +474,19 @@
     grads = front_vjp((dbeta, dgc + dgr.T))
     full = [dq, dk, dv] + [g.astype(BF) for g in grads]
 
-    def contribution(pieces):
-        total = 0.0
-        for grad_rows, weight in zip(full, pieces):
-            total = total + lax.dot_general(
-                grad_rows, weight, (((1,), (1,)), ((), ())), preferred_element_type=F32
-            )
-        return total
-
+    total = 0.0
+    for grad_rows, weight in zip(full, weights):
+        total = total + lax.dot_general(
+            grad_rows, weight, (((1,), (1,)), ((), ())), preferred_element_type=F32
+        )
     share = inputs.shape[1]
     if pair:
-        far = contribution(
-            [lax.dynamic_slice_in_dim(w, (1 - side) * share, share, 0) for w in weights]
-        ).astype(BF)
+        far = lax.dynamic_slice_in_dim(total, (1 - side) * share, share, 1).astype(BF)
         arrived = lax.ppermute(far, "tp", [(0, 1), (1, 0)])
-        near = contribution(
-            [lax.dynamic_slice_in_dim(w, side * share, share, 0) for w in weights]
-        )
+        near = lax.dynamic_slice_in_dim(total, side * share, share, 1)
         return (near + arrived.astype(F32)).astype(BF)
     return lax.psum_scatter(
-        contribution(weights).astype(BF), "tp", scatter_dimension=1, tiled=True
+        total.astype(BF), "tp", scatter_dimension=1, tiled=True
     )
 
 

time: 96.6 us -> 104 us (1.077)
  the two profiles are of different devices: /device:TPU:0 before, /device:TPU:29 now
where the time goes in v3:
time: 104 us; the launch traced here: 103 us
  Pallas kernels  65.3 us (63%)
  starting transfers between devices  18.5 us (18%)
  matrix products  8.61 us (8%)
  local copies, waits for them, and re-layouts  6.13 us (6%)
  other arithmetic  3.13 us (3%)
  waiting for transfers between devices  1.3 us (1%)
    pallas_call x1, Pallas kernels, recurrence_grads(): pl.pallas_call(functools.partial(core_kernel, kheads, ratio, group), out_...  65.3 us
    ppermute x1, starting transfers between devices, local(): arrived = lax.ppermute(far, 'tp', [(0, 1), (1, 0)])  17.7 us
    unnamed x34, local copies, waits for them, and re-layouts  5.06 us
    dot_general x5, matrix products, local(): jnp.dot(whole, w, preferred_element_type=F32).astype(BF)  4.44 us
    dot_general x5, matrix products, local(): lax.dot_general(grad_rows, weight, (((1,), (1,)), ((), ())), preferred_el...  3.79 us
  transfers between devices with their start and end apart: 2, of which 1 were waited for; matrix products, arithmetic and copies ran while one was open for 1% of the time, Pallas kernels for 0%

profile of v3, /device:TPU:29, one launch (start us, length us, event | category | flops | bytes accessed | tf_op | source)
XLA Modules:
  0.0 103.2 jit_solution(15813509065846521234)
XLA Ops:
  0.0 0.0 copy-start
  0.0 0.0 copy-start.12
  0.0 0.0 copy-start.9
  0.0 0.7 collective-permute-start
  0.8 0.7 exponential_negate_fusion
  1.4 0.7 maximum_convert_fusion.taps_ref
  2.1 0.0 copy-start.7
  2.2 0.0 collective-permute-done
  2.2 0.0 copy-start.13
  2.2 1.4 %convolution_convert_fusion.4 = bf16[128,8]{0,1:T(8,128)(2,1)S(1)} fusion(bf16[2048,8]{0,1:T(8,128)(2,1)} %param.17, bf16[128,1024]{1,0:T(8,128)(2,1)S(1)} %collective-permute-done, bf16[128,1024]{1,0:T(8,128)(2,1)} %param.12, pred[]{:T(512)S(6)} %eq.11), kind=kOutput, calls=%fused_computation.10 | convolution fusion | flops 6554624 | bytes 559105 | tf_op jit(solution)/shard_map/dot_general | solution.py:461
  3.6 0.0 copy-done.12
  3.6 0.0 copy-done.9
  3.6 0.0 copy-start.15
  3.6 0.3 convolution_convert_fusion.3
  3.9 0.1 copy-done.7
  4.0 0.0 copy-start.5
  4.0 0.4 convolution_convert_fusion.1.pk_ref
  4.5 0.0 copy-done.13
  4.5 0.0 copy-done
  4.5 0.5 convolution_convert_fusion.2.pq_ref
  4.9 1.3 %copy-done.5 = bf16[2048,1024]{1,0:T(8,128)(2,1)S(1)} copy-done((bf16[2048,1024]{1,0:T(8,128)(2,1)S(1)}, bf16[2048,1024]{1,0:T(8,128)(2,1)}, u32[]{:S(2)}) %copy-start.5) | copy-done | bytes 4194328
  6.2 0.0 copy-start.14
  6.2 0.0 copy-start.1
  6.2 1.9 %convolution_convert_fusion.pv_ref = bf16[128,1024]{1,0:T(8,128)(2,1)S(1)} fusion(bf16[2048,1024]{1,0:T(8,128)(2,1)S(1)} %copy-done.5, bf16[128,1024]{1,0:T(8,128)(2,1)} %copy-done.13, bf16[128,1024]{1,0:T(8,128)(2,1)S(1)} %copy-done.12, pred[]{:T(512)S(6)} %eq.11), kind=kOutput, calls=%fused_computation.4 | convolution fusion | flops 539361280 | bytes 4980737 | tf_op jit(solution)/shard_map/dot_general | solution.py:461
  8.1 0.0 copy-done.15
  8.1 0.0 copy-done.14
  8.1 0.2 fusion.3
  8.3 0.1 copy.14.gc_ref
  8.5 0.0 copy-done.1
  8.5 65.3 %shard_map.118 = (bf16[128,512]{1,0:T(8,128)(2,1)S(1)}, bf16[128,512]{1,0:T(8,128)(2,1)S(1)}, bf16[128,1024]{1,0:T(8,128)(2,1)S(1)}, f32[128,8]{1,0:T(8,128)S(1)...) custom-call(bf16[128,512]{1,0:T(8,128)(2,1)S(1)} %convolution_convert_fusion.2.pq_ref, ...), custom_call_target="tpu_custom_call" | custom-call | tf_op jit(solution)/shard_map/pallas_call | solution.py:400
  73.8 0.0 copy-start.2
  73.8 0.6 copy-done.2
  74.5 0.0 copy-start.4
  74.5 0.6 copy-done.4
  75.1 0.0 copy-start.16
  75.1 0.9 copy.15
  76.0 0.0 copy-start.8
  76.0 0.8 fusion.24
  76.8 0.0 copy-done.16
  76.8 0.1 fusion.1
  77.0 0.6 copy-done.8
  77.6 0.0 copy-start.6
  77.6 0.8 convolution_add_fusion.3
  78.4 1.4 %copy-done.6 = bf16[2048,1024]{1,0:T(8,128)(2,1)S(1)} copy-done((bf16[2048,1024]{1,0:T(8,128)(2,1)S(1)}, bf16[2048,1024]{1,0:T(8,128)(2,1)}, u32[]{:S(2)}) %copy-start.6) | copy-done | bytes 4194328
  79.8 0.0 copy-start.3
  79.8 0.0 copy-start.10
  79.8 1.5 %convolution_add_fusion.2 = f32[128,2048]{1,0:T(8,128)S(1)} fusion(f32[128,2048]{1,0:T(8,128)S(1)} %convolution_add_fusion.3, bf16[128,1024]{1,0:T(8,128)(2,1)S(1)} %get-tuple-element.23, bf16[2048,1024]{1,0:T(8,128)(2,1)S(1)} %copy-done.6), kind=kOutput, calls=%fused_computation.2 | convolution fusion | flops 537133056 | bytes 6553600 | tf_op jit(solution)/shard_map/dot_general | solution.py:479
  81.3 0.0 copy-start.11
  81.3 0.0 copy-done.3
  81.3 0.0 copy-done.10
  81.3 0.3 convolution_add_fusion.1
  81.6 0.4 copy-done.11
  82.1 0.3 convolution_add_fusion
  82.5 17.7 %collective-permute-start.1 = (bf16[128,1024]{1,0:T(8,128)(2,1)S(1)}, bf16[128,1024]{1,0:T(8,128)(2,1)}, u32[]{:S(2)}, u32[]{:S(2)}) collective-permute-start(bf16[128,1024]{1,0:T(8,128)(2,1)S(1)} %dynamic-slice_convert_fusion), channel_id=1, source_target_pairs={{0,1},{1,0},{2,3},{3,2},{4,5},{5,4},{6,7},{7,6},{8,9},{9,8},{10,11... | collective-permute-start | bytes 786440 | tf_op jit(solution)/shard_map/ppermute | solution.py:485
  100.2 1.3 %collective-permute-done.1 = bf16[128,1024]{1,0:T(8,128)(2,1)} collective-permute-done((bf16[128,1024]{1,0:T(8,128)(2,1)S(1)}, bf16[128,1024]{1,0:T(8,128)(2,1)}, u32[]{:S(2)}, u32[]{:S(2)}) %collective-permute-start.1) | collective-permute-done | bytes 262176 | tf_op jit(solution)/shard_map/ppermute | solution.py:485
  101.5 1.7 %add_convert_fusion = bf16[128,1024]{1,0:T(8,128)(2,1)} fusion(bf16[128,1024]{1,0:T(8,128)(2,1)} %collective-permute-done.1, f32[128,2048]{1,0:T(8,128)S(1)} %convolution_add_fusion, s32[]{:T(128)S(6)} %select_n.38), kind=kLoop, calls=%fused_computation.13 | loop fusion | flops 393216 | bytes 1048580 | tf_op jit(solution)/shard_map/convert_element_type | solution.py:487
  (2 shorter events, 0.1 us)
Async XLA Ops:
  0.0 4.5 %copy-start = (bf16[2048,512]{1,0:T(8,128)(2,1)S(1)}, bf16[2048,512]{1,0:T(8,128)(2,1)}, u32[]{:S(2)}) copy-start(bf16[2048,512]{1,0:T(8,128)(2,1)} %param.13) | copy-start | bytes 6291460
  0.0 3.6 %copy-start.12 = (bf16[128,1024]{1,0:T(8,128)(2,1)S(1)}, bf16[128,1024]{1,0:T(8,128)(2,1)}, u32[]{:S(2)}) copy-start(bf16[128,1024]{1,0:T(8,128)(2,1)} %param.12) | copy-start | bytes 786436
  0.0 3.6 %copy-start.9 = (bf16[2048,8]{0,1:T(8,128)(2,1)S(1)}, bf16[2048,8]{0,1:T(8,128)(2,1)}, u32[]{:S(2)}) copy-start(bf16[2048,8]{0,1:T(8,128)(2,1)} %param.16) | copy-start | bytes 98308
  0.0 2.1 %collective-permute-start = (bf16[128,1024]{1,0:T(8,128)(2,1)}, bf16[128,1024]{1,0:T(8,128)(2,1)S(1)}, u32[]{:S(2)}, u32[]{:S(2)}) collective-permute-start(bf16[128,1024]{1,0:T(8,128)(2,1)} %param.12), channel_id=1, source_target_pairs={{0,1},{1,0},{2,3},{3,2},{4,5},{5,4},{6,7},{7,6},{8,9},{9,8},{10,11... | collective-permute-start | bytes 786440 | tf_op jit(solution)/shard_map/ppermute | solution.py:452
  2.1 1.9 %copy-start.7 = (bf16[2048,512]{1,0:T(8,128)(2,1)S(1)}, bf16[2048,512]{1,0:T(8,128)(2,1)}, u32[]{:S(2)}) copy-start(bf16[2048,512]{1,0:T(8,128)(2,1)} %param.14) | copy-start | bytes 6291460
  2.2 2.3 %copy-start.13 = (bf16[128,1024]{1,0:T(8,128)(2,1)}, bf16[128,1024]{1,0:T(8,128)(2,1)S(1)}, u32[]{:S(2)}) copy-start(bf16[128,1024]{1,0:T(8,128)(2,1)S(1)} %collective-permute-done) | copy-start | bytes 786436
  3.6 4.5 %copy-start.15 = (bf16[128,8]{0,1:T(8,128)(2,1)}, bf16[128,8]{0,1:T(8,128)(2,1)S(1)}, u32[]{:S(2)}) copy-start(bf16[128,8]{0,1:T(8,128)(2,1)S(1)} %convolution_convert_fusion.4) | copy-start | bytes 6148
  4.0 2.2 %copy-start.5 = (bf16[2048,1024]{1,0:T(8,128)(2,1)S(1)}, bf16[2048,1024]{1,0:T(8,128)(2,1)}, u32[]{:S(2)}) copy-start(bf16[2048,1024]{1,0:T(8,128)(2,1)} %param.15) | copy-start | bytes 12582916
  6.2 1.9 %copy-start.14 = (f32[8]{0:T(128)S(1)}, f32[8]{0:T(128)}, u32[]{:S(2)}) copy-start(f32[8]{0:T(128)} %param.22) | copy-start | bytes 100
  6.2 2.3 %copy-start.1 = (bf16[128,1024]{1,0:T(8,128)(2,1)S(1)}, bf16[128,1024]{1,0:T(8,128)(2,1)}, u32[]{:S(2)}) copy-start(bf16[128,1024]{1,0:T(8,128)(2,1)} %do_ref.1) | copy-start | bytes 786436
  73.8 0.6 copy-start.2
  74.5 0.6 copy-start.4
  75.1 1.7 %copy-start.16 = (bf16[128,8]{0,1:T(8,128)(2,1)S(1)}, bf16[128,8]{0,1:T(8,128)(2,1)}, u32[]{:S(2)}) copy-start(bf16[128,8]{0,1:T(8,128)(2,1)} %copy-done.15) | copy-start | bytes 6148
  76.0 1.6 %copy-start.8 = (bf16[2048,512]{1,0:T(8,128)(2,1)S(1)}, bf16[2048,512]{1,0:T(8,128)(2,1)}, u32[]{:S(2)}) copy-start(bf16[2048,512]{1,0:T(8,128)(2,1)} %param.14) | copy-start | bytes 6291460
  77.6 2.2 %copy-start.6 = (bf16[2048,1024]{1,0:T(8,128)(2,1)S(1)}, bf16[2048,1024]{1,0:T(8,128)(2,1)}, u32[]{:S(2)}) copy-start(bf16[2048,1024]{1,0:T(8,128)(2,1)} %param.15) | copy-start | bytes 12582916
  79.8 1.5 %copy-start.3 = (f32[128,8]{1,0:T(8,128)S(1)}, f32[128,8]{1,0:T(8,128)}, u32[]{:S(2)}) copy-start(f32[128,8]{1,0:T(8,128)} %copy-done.2) | copy-start | bytes 12292
  79.8 1.5 %copy-start.10 = (bf16[2048,8]{0,1:T(8,128)(2,1)S(1)}, bf16[2048,8]{0,1:T(8,128)(2,1)}, u32[]{:S(2)}) copy-start(bf16[2048,8]{0,1:T(8,128)(2,1)} %param.16) | copy-start | bytes 98308
  81.3 0.8 copy-start.11
  82.5 19.0 %collective-permute-start.1 = (bf16[128,1024]{1,0:T(8,128)(2,1)S(1)}, bf16[128,1024]{1,0:T(8,128)(2,1)}, u32[]{:S(2)}, u32[]{:S(2)}) collective-permute-start(bf16[128,1024]{1,0:T(8,128)(2,1)S(1)} %dynamic-slice_convert_fusion), channel_id=1, source_target_pairs={{0,1},{1,0},{2,3},{3,2},{4,5},{5,4},{6,7},{7,6},{8,9},{9,8},{10,11... | collective-permute-start | bytes 786440 | tf_op jit(solution)/shard_map/ppermute | solution.py:485

commit v4 on v3

--- a/solution.py
+++ b/solution.py
@@ -228,10 +228,12 @@
             device_id_type=MESH,
         )
 
-    def advance(way, head):
+    def chain(step, carry):
+        turn, head = step // vheads, step % vheads
+        way = turn + late - 2 * turn * late
         before, after = me - 1 + 2 * way, me + 1 - 2 * way
 
-        @pl.when((before >= 0) & (before < count))
+        @pl.when((before >= 0) & (before < count) & ((turn == 0) | ((after >= 0) & (after < count))))
         def _():
             hop(way, head, before).wait_recv()
 
@@ -245,24 +247,9 @@
             ).astype(BF)
             hop(way, head, after).start()
 
-    lag = jnp.minimum(vheads, 2 * (1 - 2 * late) * (count - 1 - 2 * me))
-
-    def leading(head, carry):
-        advance(late, head)
-        return carry
-
-    def mixed(head, carry):
-        advance(1 - late, head)
-        advance(late, lag + head)
-        return carry
-
-    def trailing(head, carry):
-        advance(1 - late, head)
-        return carry
-
-    lax.fori_loop(0, lag, leading, 0)
-    lax.fori_loop(0, vheads - lag, mixed, 0)
-    lax.fori_loop(vheads - lag, vheads, trailing, 0)
+        return carry
+
+    lax.fori_loop(0, 2 * vheads, chain, 0)
 
     dbeta_ref[...] = jnp.zeros(dbeta_ref.shape, F32)
     dgc_ref[...] = jnp.zeros(dgc_ref.shape, F32)
@@ -277,6 +264,17 @@
         qk = [nt(q, k) for q, k in zip(qs, ks)]
         heads = [(i, kh[i] * ratio + r) for i in range(group) for r in range(ratio)]
         span = range(len(heads))
+
+        @pl.when(me == 0)
+        def _():
+            for _, h in heads:
+                hop(1, h, me + 1).wait_recv()
+
+        @pl.when(me == count - 1)
+        def _():
+            for _, h in heads:
+                hop(0, h, me - 1).wait_recv()
+
         gate = [gates(h) for _, h in heads]
         own_k = [ks[i] for i, _ in heads]
         own_q = [qs[i] for i, _ in heads]

time: 104 us -> 96.4 us (0.927)
  the two profiles are of different devices: /device:TPU:29 before, /device:TPU:0 now
where the time goes in v4:
time: 96.4 us; the launch traced here: 95.9 us
  Pallas kernels  75.6 us (78%)
  matrix products  8.6 us (9%)
  local copies, waits for them, and re-layouts  6.13 us (6%)
  other arithmetic  3.13 us (3%)
  waiting for transfers between devices  1.65 us (2%)
    pallas_call x1, Pallas kernels, recurrence_grads(): pl.pallas_call(functools.partial(core_kernel, kheads, ratio, group), out_...  75.6 us
    unnamed x34, local copies, waits for them, and re-layouts  5.06 us
    dot_general x5, matrix products, local(): jnp.dot(whole, w, preferred_element_type=F32).astype(BF)  4.45 us
    dot_general x5, matrix products, local(): lax.dot_general(grad_rows, weight, (((1,), (1,)), ((), ())), preferred_el...  3.78 us
  transfers between devices with their start and end apart: 2, of which 1 were waited for; matrix products, arithmetic and copies ran while one was open for 1% of the time, Pallas kernels for 0%

profile of v4, /device:TPU:0, one launch (start us, length us, event | category | flops | bytes accessed | tf_op | source)
XLA Modules:
  0.0 95.9 jit_solution(17529163009822293874)
XLA Ops:
  0.0 0.0 copy-start
  0.0 0.0 copy-start.12
  0.0 0.0 copy-start.9
  0.0 0.5 collective-permute-start
  0.5 0.7 exponential_negate_fusion
  1.2 0.7 maximum_convert_fusion.taps_ref
  1.9 0.0 copy-start.7
  1.9 0.0 collective-permute-done
  1.9 0.0 copy-start.13
  2.0 1.4 %convolution_convert_fusion.4 = bf16[128,8]{0,1:T(8,128)(2,1)S(1)} fusion(bf16[2048,8]{0,1:T(8,128)(2,1)} %param.17, bf16[128,1024]{1,0:T(8,128)(2,1)S(1)} %collective-permute-done, bf16[128,1024]{1,0:T(8,128)(2,1)} %param.12, pred[]{:T(512)S(6)} %eq.11), kind=kOutput, calls=%fused_computation.10 | convolution fusion | flops 6554624 | bytes 559105 | tf_op jit(solution)/shard_map/dot_general | solution.py:459
  3.4 0.0 copy-done.12
  3.4 0.0 copy-done.9
  3.4 0.0 copy-start.15
  3.4 0.3 convolution_convert_fusion.3
  3.7 0.1 copy-done.7
  3.8 0.0 copy-start.5
  3.8 0.4 convolution_convert_fusion.1.pk_ref
  4.2 0.0 copy-done.13
  4.2 0.0 copy-done
  4.3 0.5 convolution_convert_fusion.2.pq_ref
  4.7 1.3 %copy-done.5 = bf16[2048,1024]{1,0:T(8,128)(2,1)S(1)} copy-done((bf16[2048,1024]{1,0:T(8,128)(2,1)S(1)}, bf16[2048,1024]{1,0:T(8,128)(2,1)}, u32[]{:S(2)}) %copy-start.5) | copy-done | bytes 4194328
  6.0 0.0 copy-start.14
  6.0 0.0 copy-start.1
  6.0 1.9 %convolution_convert_fusion.pv_ref = bf16[128,1024]{1,0:T(8,128)(2,1)S(1)} fusion(bf16[2048,1024]{1,0:T(8,128)(2,1)S(1)} %copy-done.5, bf16[128,1024]{1,0:T(8,128)(2,1)} %copy-done.13, bf16[128,1024]{1,0:T(8,128)(2,1)S(1)} %copy-done.12, pred[]{:T(512)S(6)} %eq.11), kind=kOutput, calls=%fused_computation.4 | convolution fusion | flops 539361280 | bytes 4980737 | tf_op jit(solution)/shard_map/dot_general | solution.py:459
  7.8 0.0 copy-done.15
  7.8 0.0 copy-done.14
  7.9 0.2 fusion.3
  8.1 0.1 copy.14.gc_ref
  8.3 0.0 copy-done.1
  8.3 75.6 %shard_map.118 = (bf16[128,512]{1,0:T(8,128)(2,1)S(1)}, bf16[128,512]{1,0:T(8,128)(2,1)S(1)}, bf16[128,1024]{1,0:T(8,128)(2,1)S(1)}, f32[128,8]{1,0:T(8,128)S(1)...) custom-call(bf16[128,512]{1,0:T(8,128)(2,1)S(1)} %convolution_convert_fusion.2.pq_ref, ...), custom_call_target="tpu_custom_call" | custom-call | tf_op jit(solution)/shard_map/pallas_call | solution.py:398
  83.8 0.0 copy-start.2
  83.9 0.6 copy-done.2
  84.5 0.0 copy-start.4
  84.5 0.6 copy-done.4
  85.1 0.0 copy-start.16
  85.1 0.9 copy.15
  86.0 0.0 copy-start.8
  86.0 0.8 fusion.24
  86.8 0.0 copy-done.16
  86.8 0.1 fusion.1
  87.0 0.6 copy-done.8
  87.6 0.0 copy-start.6
  87.6 0.8 convolution_add_fusion.3
  88.4 1.4 %copy-done.6 = bf16[2048,1024]{1,0:T(8,128)(2,1)S(1)} copy-done((bf16[2048,1024]{1,0:T(8,128)(2,1)S(1)}, bf16[2048,1024]{1,0:T(8,128)(2,1)}, u32[]{:S(2)}) %copy-start.6) | copy-done | bytes 4194328
  89.8 0.0 copy-start.3
  89.8 0.0 copy-start.10
  89.8 1.5 %convolution_add_fusion.2 = f32[128,2048]{1,0:T(8,128)S(1)} fusion(f32[128,2048]{1,0:T(8,128)S(1)} %convolution_add_fusion.3, bf16[128,1024]{1,0:T(8,128)(2,1)S(1)} %get-tuple-element.23, bf16[2048,1024]{1,0:T(8,128)(2,1)S(1)} %copy-done.6), kind=kOutput, calls=%fused_computation.2 | convolution fusion | flops 537133056 | bytes 6553600 | tf_op jit(solution)/shard_map/dot_general | solution.py:477
  91.3 0.0 copy-start.11
  91.3 0.0 copy-done.3
  91.3 0.0 copy-done.10
  91.4 0.3 convolution_add_fusion.1
  91.7 0.4 copy-done.11
  92.1 0.3 convolution_add_fusion
  92.5 0.1 collective-permute-start.1
  92.6 1.6 %collective-permute-done.1 = bf16[128,1024]{1,0:T(8,128)(2,1)} collective-permute-done((bf16[128,1024]{1,0:T(8,128)(2,1)S(1)}, bf16[128,1024]{1,0:T(8,128)(2,1)}, u32[]{:S(2)}, u32[]{:S(2)}) %collective-permute-start.1) | collective-permute-done | bytes 262176 | tf_op jit(solution)/shard_map/ppermute | solution.py:483
  94.2 1.7 %add_convert_fusion = bf16[128,1024]{1,0:T(8,128)(2,1)} fusion(bf16[128,1024]{1,0:T(8,128)(2,1)} %collective-permute-done.1, f32[128,2048]{1,0:T(8,128)S(1)} %convolution_add_fusion, s32[]{:T(128)S(6)} %select_n.38), kind=kLoop, calls=%fused_computation.13 | loop fusion | flops 393216 | bytes 1048580 | tf_op jit(solution)/shard_map/convert_element_type | solution.py:485
  (2 shorter events, 0.1 us)
Async XLA Ops:
  0.0 4.2 %copy-start = (bf16[2048,512]{1,0:T(8,128)(2,1)S(1)}, bf16[2048,512]{1,0:T(8,128)(2,1)}, u32[]{:S(2)}) copy-start(bf16[2048,512]{1,0:T(8,128)(2,1)} %param.13) | copy-start | bytes 6291460
  0.0 3.4 %copy-start.12 = (bf16[128,1024]{1,0:T(8,128)(2,1)S(1)}, bf16[128,1024]{1,0:T(8,128)(2,1)}, u32[]{:S(2)}) copy-start(bf16[128,1024]{1,0:T(8,128)(2,1)} %param.12) | copy-start | bytes 786436
  0.0 3.4 %copy-start.9 = (bf16[2048,8]{0,1:T(8,128)(2,1)S(1)}, bf16[2048,8]{0,1:T(8,128)(2,1)}, u32[]{:S(2)}) copy-start(bf16[2048,8]{0,1:T(8,128)(2,1)} %param.16) | copy-start | bytes 98308
  0.0 1.9 %collective-permute-start = (bf16[128,1024]{1,0:T(8,128)(2,1)}, bf16[128,1024]{1,0:T(8,128)(2,1)S(1)}, u32[]{:S(2)}, u32[]{:S(2)}) collective-permute-start(bf16[128,1024]{1,0:T(8,128)(2,1)} %param.12), channel_id=1, source_target_pairs={{0,1},{1,0},{2,3},{3,2},{4,5},{5,4},{6,7},{7,6},{8,9},{9,8},{10,11... | collective-permute-start | bytes 786440 | tf_op jit(solution)/shard_map/ppermute | solution.py:450
  1.9 1.9 %copy-start.7 = (bf16[2048,512]{1,0:T(8,128)(2,1)S(1)}, bf16[2048,512]{1,0:T(8,128)(2,1)}, u32[]{:S(2)}) copy-start(bf16[2048,512]{1,0:T(8,128)(2,1)} %param.14) | copy-start | bytes 6291460
  1.9 2.3 %copy-start.13 = (bf16[128,1024]{1,0:T(8,128)(2,1)}, bf16[128,1024]{1,0:T(8,128)(2,1)S(1)}, u32[]{:S(2)}) copy-start(bf16[128,1024]{1,0:T(8,128)(2,1)S(1)} %collective-permute-done) | copy-start | bytes 786436
  3.4 4.5 %copy-start.15 = (bf16[128,8]{0,1:T(8,128)(2,1)}, bf16[128,8]{0,1:T(8,128)(2,1)S(1)}, u32[]{:S(2)}) copy-start(bf16[128,8]{0,1:T(8,128)(2,1)S(1)} %convolution_convert_fusion.4) | copy-start | bytes 6148
  3.8 2.2 %copy-start.5 = (bf16[2048,1024]{1,0:T(8,128)(2,1)S(1)}, bf16[2048,1024]{1,0:T(8,128)(2,1)}, u32[]{:S(2)}) copy-start(bf16[2048,1024]{1,0:T(8,128)(2,1)} %param.15) | copy-start | bytes 12582916
  6.0 1.9 %copy-start.14 = (f32[8]{0:T(128)S(1)}, f32[8]{0:T(128)}, u32[]{:S(2)}) copy-start(f32[8]{0:T(128)} %param.22) | copy-start | bytes 100
  6.0 2.3 %copy-start.1 = (bf16[128,1024]{1,0:T(8,128)(2,1)S(1)}, bf16[128,1024]{1,0:T(8,128)(2,1)}, u32[]{:S(2)}) copy-start(bf16[128,1024]{1,0:T(8,128)(2,1)} %do_ref.1) | copy-start | bytes 786436
  83.8 0.6 copy-start.2
  84.5 0.6 copy-start.4
  85.1 1.7 %copy-start.16 = (bf16[128,8]{0,1:T(8,128)(2,1)S(1)}, bf16[128,8]{0,1:T(8,128)(2,1)}, u32[]{:S(2)}) copy-start(bf16[128,8]{0,1:T(8,128)(2,1)} %copy-done.15) | copy-start | bytes 6148
  86.0 1.6 %copy-start.8 = (bf16[2048,512]{1,0:T(8,128)(2,1)S(1)}, bf16[2048,512]{1,0:T(8,128)(2,1)}, u32[]{:S(2)}) copy-start(bf16[2048,512]{1,0:T(8,128)(2,1)} %param.14) | copy-start | bytes 6291460
  87.6 2.2 %copy-start.6 = (bf16[2048,1024]{1,0:T(8,128)(2,1)S(1)}, bf16[2048,1024]{1,0:T(8,128)(2,1)}, u32[]{:S(2)}) copy-start(bf16[2048,1024]{1,0:T(8,128)(2,1)} %param.15) | copy-start | bytes 12582916
  89.8 1.5 %copy-start.3 = (f32[128,8]{1,0:T(8,128)S(1)}, f32[128,8]{1,0:T(8,128)}, u32[]{:S(2)}) copy-start(f32[128,8]{1,0:T(8,128)} %copy-done.2) | copy-start | bytes 12292
  89.8 1.5 %copy-start.10 = (bf16[2048,8]{0,1:T(8,128)(2,1)S(1)}, bf16[2048,8]{0,1:T(8,128)(2,1)}, u32[]{:S(2)}) copy-start(bf16[2048,8]{0,1:T(8,128)(2,1)} %param.16) | copy-start | bytes 98308
  91.3 0.8 copy-start.11
  92.5 1.7 %collective-permute-start.1 = (bf16[128,1024]{1,0:T(8,128)(2,1)S(1)}, bf16[128,1024]{1,0:T(8,128)(2,1)}, u32[]{:S(2)}, u32[]{:S(2)}) collective-permute-start(bf16[128,1024]{1,0:T(8,128)(2,1)S(1)} %dynamic-slice_convert_fusion), channel_id=1, source_target_pairs={{0,1},{1,0},{2,3},{3,2},{4,5},{5,4},{6,7},{7,6},{8,9},{9,8},{10,11... | collective-permute-start | bytes 786440 | tf_op jit(solution)/shard_map/ppermute | solution.py:483

commit v5 on v4

--- a/solution.py
+++ b/solution.py
@@ -160,8 +160,8 @@
         v_ref[:, lane_block(head)] = total * gate
         return carry
 
-    lax.fori_loop(0, kheads, front_qk, 0)
-    lax.fori_loop(0, vheads, front_v, 0)
+    lax.fori_loop(0, kheads, front_qk, 0, unroll=True)
+    lax.fori_loop(0, vheads, front_v, 0, unroll=True)
 
     def front_back(block, grad, scale):
         total, gate = convolved(block)
@@ -341,7 +341,7 @@
         dpad_s[:, lanes] = total
         return carry
 
-    lax.fori_loop(0, width // DH, transposed, 0)
+    lax.fori_loop(0, width // DH, transposed, 0, unroll=True)
 
     @pl.when(me > 0)
     def _():

time: 96.4 us -> 95.9 us (level)
  no operation moved by 1% of the time
where the time goes in v5:
time: 95.9 us; the launch traced here: 95.4 us
  Pallas kernels  75.1 us (78%)
  matrix products  8.61 us (9%)
  local copies, waits for them, and re-layouts  6.13 us (6%)
  other arithmetic  3.13 us (3%)
  waiting for transfers between devices  1.65 us (2%)
    pallas_call x1, Pallas kernels, recurrence_grads(): pl.pallas_call(functools.partial(core_kernel, kheads, ratio, group), out_...  75.1 us
    unnamed x34, local copies, waits for them, and re-layouts  5.07 us
    dot_general x5, matrix products, local(): jnp.dot(whole, w, preferred_element_type=F32).astype(BF)  4.45 us
    dot_general x5, matrix products, local(): lax.dot_general(grad_rows, weight, (((1,), (1,)), ((), ())), preferred_el...  3.79 us
  transfers between devices with their start and end apart: 2, of which 1 were waited for; matrix products, arithmetic and copies ran while one was open for 1% of the time, Pallas kernels for 0%

profile of v5, /device:TPU:0, one launch (start us, length us, event | category | flops | bytes accessed | tf_op | source)
XLA Modules:
  0.0 95.4 jit_solution(2707285946803310295)
XLA Ops:
  0.0 0.0 copy-start
  0.0 0.0 copy-start.12
  0.0 0.0 copy-start.9
  0.0 0.5 collective-permute-start
  0.5 0.7 exponential_negate_fusion
  1.2 0.7 maximum_convert_fusion.taps_ref
  1.9 0.0 copy-start.7
  1.9 0.0 collective-permute-done
  1.9 0.0 copy-start.13
  2.0 1.4 %convolution_convert_fusion.4 = bf16[128,8]{0,1:T(8,128)(2,1)S(1)} fusion(bf16[2048,8]{0,1:T(8,128)(2,1)} %param.17, bf16[128,1024]{1,0:T(8,128)(2,1)S(1)} %collective-permute-done, bf16[128,1024]{1,0:T(8,128)(2,1)} %param.12, pred[]{:T(512)S(6)} %eq.11), kind=kOutput, calls=%fused_computation.10 | convolution fusion | flops 6554624 | bytes 559105 | tf_op jit(solution)/shard_map/dot_general | solution.py:459
  3.4 0.0 copy-done.12
  3.4 0.0 copy-done.9
  3.4 0.0 copy-start.15
  3.4 0.3 convolution_convert_fusion.3
  3.7 0.1 copy-done.7
  3.8 0.0 copy-start.5
  3.8 0.4 convolution_convert_fusion.1.pk_ref
  4.2 0.0 copy-done.13
  4.2 0.0 copy-done
  4.3 0.5 convolution_convert_fusion.2.pq_ref
  4.7 1.3 %copy-done.5 = bf16[2048,1024]{1,0:T(8,128)(2,1)S(1)} copy-done((bf16[2048,1024]{1,0:T(8,128)(2,1)S(1)}, bf16[2048,1024]{1,0:T(8,128)(2,1)}, u32[]{:S(2)}) %copy-start.5) | copy-done | bytes 4194328
  6.0 0.0 copy-start.14
  6.0 0.0 copy-start.1
  6.0 1.9 %convolution_convert_fusion.pv_ref = bf16[128,1024]{1,0:T(8,128)(2,1)S(1)} fusion(bf16[2048,1024]{1,0:T(8,128)(2,1)S(1)} %copy-done.5, bf16[128,1024]{1,0:T(8,128)(2,1)} %copy-done.13, bf16[128,1024]{1,0:T(8,128)(2,1)S(1)} %copy-done.12, pred[]{:T(512)S(6)} %eq.11), kind=kOutput, calls=%fused_computation.4 | convolution fusion | flops 539361280 | bytes 4980737 | tf_op jit(solution)/shard_map/dot_general | solution.py:459
  7.8 0.0 copy-done.15
  7.8 0.0 copy-done.14
  7.9 0.2 fusion.3
  8.1 0.1 copy.14.gc_ref
  8.3 0.0 copy-done.1
  8.3 75.1 %shard_map.118 = (bf16[128,512]{1,0:T(8,128)(2,1)S(1)}, bf16[128,512]{1,0:T(8,128)(2,1)S(1)}, bf16[128,1024]{1,0:T(8,128)(2,1)S(1)}, f32[128,8]{1,0:T(8,128)S(1)...) custom-call(bf16[128,512]{1,0:T(8,128)(2,1)S(1)} %convolution_convert_fusion.2.pq_ref, ...), custom_call_target="tpu_custom_call" | custom-call | tf_op jit(solution)/shard_map/pallas_call | solution.py:398
  83.3 0.0 copy-start.2
  83.3 0.6 copy-done.2
  84.0 0.0 copy-start.4
  84.0 0.6 copy-done.4
  84.6 0.0 copy-start.16
  84.6 0.9 copy.15
  85.5 0.0 copy-start.8
  85.5 0.8 fusion.24
  86.3 0.0 copy-done.16
  86.3 0.1 fusion.1
  86.5 0.6 copy-done.8
  87.1 0.0 copy-start.6
  87.1 0.8 convolution_add_fusion.3
  87.9 1.4 %copy-done.6 = bf16[2048,1024]{1,0:T(8,128)(2,1)S(1)} copy-done((bf16[2048,1024]{1,0:T(8,128)(2,1)S(1)}, bf16[2048,1024]{1,0:T(8,128)(2,1)}, u32[]{:S(2)}) %copy-start.6) | copy-done | bytes 4194328
  89.3 0.0 copy-start.3
  89.3 0.0 copy-start.10
  89.3 1.5 %convolution_add_fusion.2 = f32[128,2048]{1,0:T(8,128)S(1)} fusion(f32[128,2048]{1,0:T(8,128)S(1)} %convolution_add_fusion.3, bf16[128,1024]{1,0:T(8,128)(2,1)S(1)} %get-tuple-element.23, bf16[2048,1024]{1,0:T(8,128)(2,1)S(1)} %copy-done.6), kind=kOutput, calls=%fused_computation.2 | convolution fusion | flops 537133056 | bytes 6553600 | tf_op jit(solution)/shard_map/dot_general | solution.py:477
  90.8 0.0 copy-start.11
  90.8 0.0 copy-done.3
  90.8 0.0 copy-done.10
  90.8 0.3 convolution_add_fusion.1
  91.2 0.4 copy-done.11
  91.6 0.3 convolution_add_fusion
  92.0 0.1 collective-permute-start.1
  92.1 1.6 %collective-permute-done.1 = bf16[128,1024]{1,0:T(8,128)(2,1)} collective-permute-done((bf16[128,1024]{1,0:T(8,128)(2,1)S(1)}, bf16[128,1024]{1,0:T(8,128)(2,1)}, u32[]{:S(2)}, u32[]{:S(2)}) %collective-permute-start.1) | collective-permute-done | bytes 262176 | tf_op jit(solution)/shard_map/ppermute | solution.py:483
  93.7 1.7 %add_convert_fusion = bf16[128,1024]{1,0:T(8,128)(2,1)} fusion(bf16[128,1024]{1,0:T(8,128)(2,1)} %collective-permute-done.1, f32[128,2048]{1,0:T(8,128)S(1)} %convolution_add_fusion, s32[]{:T(128)S(6)} %select_n.38), kind=kLoop, calls=%fused_computation.13 | loop fusion | flops 393216 | bytes 1048580 | tf_op jit(solution)/shard_map/convert_element_type | solution.py:485
  (2 shorter events, 0.1 us)
Async XLA Ops:
  0.0 4.2 %copy-start = (bf16[2048,512]{1,0:T(8,128)(2,1)S(1)}, bf16[2048,512]{1,0:T(8,128)(2,1)}, u32[]{:S(2)}) copy-start(bf16[2048,512]{1,0:T(8,128)(2,1)} %param.13) | copy-start | bytes 6291460
  0.0 3.4 %copy-start.12 = (bf16[128,1024]{1,0:T(8,128)(2,1)S(1)}, bf16[128,1024]{1,0:T(8,128)(2,1)}, u32[]{:S(2)}) copy-start(bf16[128,1024]{1,0:T(8,128)(2,1)} %param.12) | copy-start | bytes 786436
  0.0 3.4 %copy-start.9 = (bf16[2048,8]{0,1:T(8,128)(2,1)S(1)}, bf16[2048,8]{0,1:T(8,128)(2,1)}, u32[]{:S(2)}) copy-start(bf16[2048,8]{0,1:T(8,128)(2,1)} %param.16) | copy-start | bytes 98308
  0.0 1.9 %collective-permute-start = (bf16[128,1024]{1,0:T(8,128)(2,1)}, bf16[128,1024]{1,0:T(8,128)(2,1)S(1)}, u32[]{:S(2)}, u32[]{:S(2)}) collective-permute-start(bf16[128,1024]{1,0:T(8,128)(2,1)} %param.12), channel_id=1, source_target_pairs={{0,1},{1,0},{2,3},{3,2},{4,5},{5,4},{6,7},{7,6},{8,9},{9,8},{10,11... | collective-permute-start | bytes 786440 | tf_op jit(solution)/shard_map/ppermute | solution.py:450
  1.9 1.9 %copy-start.7 = (bf16[2048,512]{1,0:T(8,128)(2,1)S(1)}, bf16[2048,512]{1,0:T(8,128)(2,1)}, u32[]{:S(2)}) copy-start(bf16[2048,512]{1,0:T(8,128)(2,1)} %param.14) | copy-start | bytes 6291460
  1.9 2.3 %copy-start.13 = (bf16[128,1024]{1,0:T(8,128)(2,1)}, bf16[128,1024]{1,0:T(8,128)(2,1)S(1)}, u32[]{:S(2)}) copy-start(bf16[128,1024]{1,0:T(8,128)(2,1)S(1)} %collective-permute-done) | copy-start | bytes 786436
  3.4 4.5 %copy-start.15 = (bf16[128,8]{0,1:T(8,128)(2,1)}, bf16[128,8]{0,1:T(8,128)(2,1)S(1)}, u32[]{:S(2)}) copy-start(bf16[128,8]{0,1:T(8,128)(2,1)S(1)} %convolution_convert_fusion.4) | copy-start | bytes 6148
  3.8 2.2 %copy-start.5 = (bf16[2048,1024]{1,0:T(8,128)(2,1)S(1)}, bf16[2048,1024]{1,0:T(8,128)(2,1)}, u32[]{:S(2)}) copy-start(bf16[2048,1024]{1,0:T(8,128)(2,1)} %param.15) | copy-start | bytes 12582916
  6.0 1.9 %copy-start.14 = (f32[8]{0:T(128)S(1)}, f32[8]{0:T(128)}, u32[]{:S(2)}) copy-start(f32[8]{0:T(128)} %param.22) | copy-start | bytes 100
  6.0 2.3 %copy-start.1 = (bf16[128,1024]{1,0:T(8,128)(2,1)S(1)}, bf16[128,1024]{1,0:T(8,128)(2,1)}, u32[]{:S(2)}) copy-start(bf16[128,1024]{1,0:T(8,128)(2,1)} %do_ref.1) | copy-start | bytes 786436
  83.3 0.6 copy-start.2
  84.0 0.6 copy-start.4
  84.6 1.7 %copy-start.16 = (bf16[128,8]{0,1:T(8,128)(2,1)S(1)}, bf16[128,8]{0,1:T(8,128)(2,1)}, u32[]{:S(2)}) copy-start(bf16[128,8]{0,1:T(8,128)(2,1)} %copy-done.15) | copy-start | bytes 6148
  85.5 1.6 %copy-start.8 = (bf16[2048,512]{1,0:T(8,128)(2,1)S(1)}, bf16[2048,512]{1,0:T(8,128)(2,1)}, u32[]{:S(2)}) copy-start(bf16[2048,512]{1,0:T(8,128)(2,1)} %param.14) | copy-start | bytes 6291460
  87.1 2.2 %copy-start.6 = (bf16[2048,1024]{1,0:T(8,128)(2,1)S(1)}, bf16[2048,1024]{1,0:T(8,128)(2,1)}, u32[]{:S(2)}) copy-start(bf16[2048,1024]{1,0:T(8,128)(2,1)} %param.15) | copy-start | bytes 12582916
  89.3 1.5 %copy-start.3 = (f32[128,8]{1,0:T(8,128)S(1)}, f32[128,8]{1,0:T(8,128)}, u32[]{:S(2)}) copy-start(f32[128,8]{1,0:T(8,128)} %copy-done.2) | copy-start | bytes 12292
  89.3 1.5 %copy-start.10 = (bf16[2048,8]{0,1:T(8,128)(2,1)S(1)}, bf16[2048,8]{0,1:T(8,128)(2,1)}, u32[]{:S(2)}) copy-start(bf16[2048,8]{0,1:T(8,128)(2,1)} %param.16) | copy-start | bytes 98308
  90.8 0.8 copy-start.11
  92.0 1.7 %collective-permute-start.1 = (bf16[128,1024]{1,0:T(8,128)(2,1)S(1)}, bf16[128,1024]{1,0:T(8,128)(2,1)}, u32[]{:S(2)}, u32[]{:S(2)}) collective-permute-start(bf16[128,1024]{1,0:T(8,128)(2,1)S(1)} %dynamic-slice_convert_fusion), channel_id=1, source_target_pairs={{0,1},{1,0},{2,3},{3,2},{4,5},{5,4},{6,7},{7,6},{8,9},{9,8},{10,11... | collective-permute-start | bytes 786440 | tf_op jit(solution)/shard_map/ppermute | solution.py:483
